TPU v7x, 32 devices: a whole 2x2x4 slice. The times are simulated.
32 devices in a mesh: loop: 8 (over z, core), chan: 4 (over y, x).
Axes of the slice: x: 2, y: 2, z: 4, core: 2. Of those that a mesh axis runs over, the one named last changes fastest.
Arguments:
- features: bfloat16 [32768, 256], P('loop', 'chan'), may hold values from -6 to 6
- kernel_tap_rows: float32 [9, 256], P(None, 'chan'), may hold values from -2 to 2
- in_weight: bfloat16 [256, 1024], replicated, may hold values from -0.375 to 0.375
- out_weight: bfloat16 [1024, 256], replicated, may hold values from -0.1875 to 0.1875
- cotangent: bfloat16 [32768, 256], P('loop', 'chan'), may hold values from -6 to 6
Outputs:
- block_out: bfloat16 [32768, 256], P('loop', 'chan')
- grad_features: bfloat16 [32768, 256], P('loop', 'chan')
- grad_in_weight: float32 [256, 1024], P('chan', 'loop')
- grad_out_weight: float32 [1024, 256], P('loop', 'chan')
- grad_kernel: float32 [9, 256], P(None, 'chan')
All inputs are finite; a program needn't handle non-finite values.
Results may differ from a plain program's by a relative error of at most 0.017.
Values may be sent and summed in bfloat16 or wider, within the bound.
A program may use at most 64 MiB of HBM per device.

v0:
```python
import functools
import math

import jax
import jax.numpy as jnp
from jax import lax
from jax.experimental import pallas as pl
from jax.experimental.pallas import tpu as pltpu
from jax.sharding import PartitionSpec as P

TAPS = 9
DILATION_STEP = 512


gelu_scale = math.sqrt(2.0 / math.pi)
cubic_coef = 0.044715
epsilon = 1e-05


def with_halo(cells, sides, width):
    for axis, dim in sides:
        count = lax.axis_size(axis)
        head = lax.slice_in_dim(cells, 0, width, axis=dim)
        tail = lax.slice_in_dim(cells, cells.shape[dim] - width, cells.shape[dim], axis=dim)
        cells = jnp.concatenate(
            [
                lax.ppermute(tail, axis, [(i, (i + 1) % count) for i in range(count)]),
                cells,
                lax.ppermute(head, axis, [((i + 1) % count, i) for i in range(count)]),
            ],
            axis=dim,
        )
    return cells


def gelu_pair(inputs):
    inner_arg = gelu_scale * (inputs + cubic_coef * inputs * inputs * inputs)
    tangent = jnp.tanh(inner_arg)
    act_value = 0.5 * inputs * (1.0 + tangent)
    act_slope = 0.5 * (1.0 + tangent) + 0.5 * inputs * (1.0 - tangent * tangent) * gelu_scale * (
        1.0 + 3.0 * cubic_coef * inputs * inputs
    )
    return (act_value, act_slope)


def widen_rows(field_rows, reach_positions):
    return with_halo(field_rows, (("loop", 0),), reach_positions)


def shards(features, kernel_tap_rows, in_weight, out_weight, cotangent):
    middle_position = (TAPS - 1) // 2
    reach_positions = middle_position * DILATION_STEP
    loop_size = lax.axis_size("loop")
    chan_size = lax.axis_size("chan")
    rows_here = features.shape[0]
    grad_scale = 1.0 / math.sqrt(rows_here * loop_size)
    padded_in = widen_rows(features, reach_positions)
    blended_sum = jnp.zeros(features.shape, jnp.float32)
    for kernel_tap_index in range(TAPS):
        leading_row = reach_positions + (kernel_tap_index - middle_position) * DILATION_STEP
        blended_sum = blended_sum + kernel_tap_rows[kernel_tap_index] * padded_in[
            leading_row : leading_row + rows_here
        ].astype(jnp.float32)
    filtered = blended_sum.astype(jnp.bfloat16)
    row_block, upstream = (
        lax.all_to_all(filtered, "chan", split_axis=0, concat_axis=1, tiled=True),
        lax.all_to_all(cotangent, "chan", split_axis=0, concat_axis=1, tiled=True),
    )
    values = row_block.astype(jnp.float32)
    mean_value = jnp.mean(values, axis=-1, keepdims=True)
    centred = values - mean_value
    variance = jnp.mean(centred * centred, axis=-1, keepdims=True)
    inv_std = lax.rsqrt(variance + epsilon)
    normed = centred * inv_std
    normed_b = normed.astype(jnp.bfloat16)
    hidden_pre = jnp.dot(normed_b, in_weight, preferred_element_type=jnp.float32)
    act_value, act_slope = gelu_pair(hidden_pre)
    act_b = act_value.astype(jnp.bfloat16)
    branch = jnp.dot(act_b, out_weight, preferred_element_type=jnp.float32).astype(jnp.bfloat16)
    grad_act = jnp.einsum("pc,fc->pf", upstream, out_weight, preferred_element_type=jnp.float32)
    grad_pre = (grad_act * act_slope).astype(jnp.bfloat16)
    grad_normed = jnp.einsum("pf,cf->pc", grad_pre, in_weight, preferred_element_type=jnp.float32)
    grad_filtered = inv_std * (
        grad_normed
        - jnp.mean(grad_normed, axis=-1, keepdims=True)
        - normed * jnp.mean(grad_normed * normed, axis=-1, keepdims=True)
    )
    back_rows = grad_filtered.astype(jnp.bfloat16)
    local_rows = row_block.shape[0]
    width_c = row_block.shape[1]
    width_f = hidden_pre.shape[1]
    chan_part = width_c // chan_size
    loop_part = width_f // loop_size
    normed_parts = normed_b.reshape(local_rows, chan_size, chan_part)
    upstream_parts = upstream.reshape(local_rows, chan_size, chan_part)
    grad_parts = grad_pre.reshape(local_rows, loop_size, loop_part)
    act_parts = act_b.reshape(local_rows, loop_size, loop_part)
    term_in = (
        jnp.einsum("pai,pbj->baij", normed_parts, grad_parts, preferred_element_type=jnp.float32)
        * grad_scale
    )
    term_out = (
        jnp.einsum("pbj,pai->baji", act_parts, upstream_parts, preferred_element_type=jnp.float32)
        * grad_scale
    )
    branch_cols, back_cols = (
        lax.all_to_all(branch, "chan", split_axis=1, concat_axis=0, tiled=True),
        lax.all_to_all(back_rows, "chan", split_axis=1, concat_axis=0, tiled=True),
    )
    block_out = (features.astype(jnp.float32) + branch_cols.astype(jnp.float32)).astype(
        jnp.bfloat16
    )
    first_in, first_out = (
        lax.psum_scatter(
            term_in.astype(jnp.bfloat16), "chan", scatter_dimension=1, tiled=True
        ).astype(jnp.float32),
        lax.psum_scatter(
            term_out.astype(jnp.bfloat16), "chan", scatter_dimension=1, tiled=True
        ).astype(jnp.float32),
    )
    summed_in, summed_out = (
        lax.psum_scatter(first_in, "loop", scatter_dimension=0, tiled=True),
        lax.psum_scatter(first_out, "loop", scatter_dimension=0, tiled=True),
    )
    grad_in_weight = summed_in.reshape(chan_part, loop_part)
    grad_out_weight = summed_out.reshape(loop_part, chan_part)
    padded_back = widen_rows(back_cols, reach_positions)
    grad_sum_rows = cotangent.astype(jnp.float32)
    back_wide = back_cols.astype(jnp.float32)
    kernel_rows = []
    for kernel_tap_index in range(TAPS):
        shift_positions = (kernel_tap_index - middle_position) * DILATION_STEP
        first_back = reach_positions - shift_positions
        grad_sum_rows = grad_sum_rows + kernel_tap_rows[kernel_tap_index] * padded_back[
            first_back : first_back + rows_here
        ].astype(jnp.float32)
        first_in_row = reach_positions + shift_positions
        kernel_rows.append(
            jnp.sum(
                back_wide * padded_in[first_in_row : first_in_row + rows_here].astype(jnp.float32),
                axis=0,
            )
        )
    kernel_terms = jnp.stack(kernel_rows) * grad_scale
    grad_kernel = lax.psum(kernel_terms, "loop")
    return (
        block_out,
        grad_sum_rows.astype(jnp.bfloat16),
        grad_in_weight,
        grad_out_weight,
        grad_kernel,
    )


MESH = pl.DeviceIdType.MESH
MIDDLE = (TAPS - 1) // 2
TILE_STEPS = 2


def fused_kernel(
    L, J, grad_scale,
    x, ct, taps, win, wout,
    bo_out, gx_out, gw_in_out, gw_out_out, gk_out,
    tb, tf, wint, woutt, xs, xe, cs, ctf, xr, nb, nrm, istd, act, gp, ge,
    bs, br, gs, gr, gfull, gsend, grecv, hf, hs, hr, sf, tr, kp, kr, kt,
    send, recv,
):
    cl, rows = x.shape
    C = cl * J
    F = win.shape[1]
    R = DILATION_STEP // J
    K = rows // DILATION_STEP
    PAIRS = K // 2
    TILE = 2 * R
    Z = L // 2
    own = MIDDLE * R
    me_l, me_j = lax.axis_index("loop"), lax.axis_index("chan")
    core, z = lax.rem(me_l, 2), me_l // 2
    used = [0]

    def take(n=1):
        used[0] += n
        return used[0] - n

    def rcopy(src, dst, idx, l, j):
        return pltpu.make_async_remote_copy(
            src_ref=src, dst_ref=dst, send_sem=send.at[idx], recv_sem=recv.at[idx],
            device_id=(l, j), device_id_type=MESH)

    chan_peers = [lax.rem(me_j + d, J) for d in range(1, J)]
    loop_peers = [lax.rem(me_l + e, L) for e in range(1, L)]
    right, left = loop_peers[0], loop_peers[-1]

    barrier = pltpu.get_barrier_semaphore()
    for j in chan_peers:
        pl.semaphore_signal(barrier, inc=1, device_id=(me_l, j), device_id_type=MESH)
    for l in loop_peers:
        pl.semaphore_signal(barrier, inc=1, device_id=(l, me_j), device_id_type=MESH)

    def pack(src, dst):
        for k in range(K):
            for j in range(J):
                a = k * DILATION_STEP + j * R
                dst[j, :, k * R:(k + 1) * R] = src[:, a:a + R]

    tb[me_j] = jnp.zeros((16, 128), jnp.float32)
    tb[me_j, 0:TAPS, 0:cl] = taps[...]
    pack(x, xs)
    pl.semaphore_wait(barrier, J - 1 + L - 1)

    pending = []

    def to_chan(src, dst):
        out = []
        for j in chan_peers:
            c = rcopy(src.at[j], dst.at[me_j], take(), me_l, j)
            c.start()
            out.append(c)
        pending.extend(out)
        return out

    x_in = to_chan(xs, xr)
    tap_in = []
    for j in chan_peers:
        c = rcopy(tb.at[me_j], tb.at[me_j], take(), me_l, j)
        c.start()
        tap_in.append(c)
    pending.extend(tap_in)
    pack(ct, cs)
    ct_in = to_chan(cs, ctf)

    wint[...] = win[...].T
    woutt[...] = wout[...].T
    xr[me_j] = xs[me_j]
    for c in x_in:
        c.wait_recv()
    for s in range(J):
        xe[s * cl:(s + 1) * cl, own:own + K * R] = xr[s]
    x_left = rcopy(xe.at[:, own:own + own], xe.at[:, own + K * R:2 * own + K * R], take(), left, me_j)
    x_left.start()
    x_right = rcopy(xe.at[:, K * R:own + K * R], xe.at[:, 0:own], take(), right, me_j)
    x_right.start()
    for c in tap_in:
        c.wait_recv()
    columns = jnp.concatenate(
        [jnp.concatenate([tb[s, :, 0:cl] for s in range(J)], axis=1), jnp.zeros((112, C), jnp.float32)], axis=0).T
    for t in range(TAPS):
        tf[t] = jnp.broadcast_to(columns[:, t:t + 1], (C, R))
    ctf[me_j] = cs[me_j]
    for c in ct_in:
        c.wait_recv()
    x_left.wait_recv()
    x_right.wait_recv()
    pending.extend([x_left, x_right])

    bo_base = take(PAIRS * (J - 1))
    ge_left = rcopy(ge.at[:, own:own + own], ge.at[:, own + K * R:2 * own + K * R], take(), left, me_j)
    ge_right = rcopy(ge.at[:, K * R:own + K * R], ge.at[:, 0:own], take(), right, me_j)
    gs_base = take(PAIRS * (J - 1))
    core_base = take(Z)

    def tile_sends(src, dst, base, tile):
        at = pl.ds(pl.multiple_of(tile * TILE, TILE), TILE)
        return [rcopy(src.at[j, :, at], dst.at[me_j, :, at], base + tile * (J - 1) + d, me_l, j)
                for d, j in enumerate(chan_peers)]

    def tile_body(tile, carry):
        base = pl.multiple_of(tile * TILE, TILE)
        for b in range(TILE_STEPS):
            for j in range(J):
                ch = slice(j * cl, (j + 1) * cl)
                acc = jnp.zeros((cl, R), jnp.float32)
                for t in range(TAPS):
                    acc = acc + tf[t, ch, :] * xe[ch, pl.ds(base + (b + t) * R, R)].astype(jnp.float32)
                nrm[ch, b * R:(b + 1) * R] = acc.astype(jnp.bfloat16).astype(jnp.float32)
            here_b = slice(b * R, (b + 1) * R)
            v = nrm[:, here_b]
            centred = v - jnp.mean(v, axis=0, keepdims=True)
            inv = lax.rsqrt(jnp.mean(centred * centred, axis=0, keepdims=True) + epsilon)
            normed = centred * inv
            nrm[:, here_b] = normed
            istd[:, here_b] = inv
            nb[:, pl.ds(base + b * R, R)] = normed.astype(jnp.bfloat16)
        here = pl.ds(base, TILE)
        normed_b = nb[:, here]
        up = jnp.concatenate([ctf[j, :, here] for j in range(J)], axis=0)
        FC = 256
        for f in range(F // FC):
            part = slice(f * FC, (f + 1) * FC)
            pre = jnp.dot(wint[part, :], normed_b, preferred_element_type=jnp.float32)
            ga = jnp.dot(wout[part, :], up, preferred_element_type=jnp.float32)
            sq = pre * pre
            tangent = jnp.tanh(pre * (gelu_scale + (gelu_scale * cubic_coef) * sq))
            gate = 0.5 + 0.5 * tangent
            slope = gate + pre * (gate * (1.0 - tangent)) * (gelu_scale + (3.0 * gelu_scale * cubic_coef) * sq)
            act[part, here] = (pre * gate).astype(jnp.bfloat16)
            gp[part, here] = (ga * slope).astype(jnp.bfloat16)
        gn = jnp.dot(win[...], gp[:, here], preferred_element_type=jnp.float32)
        for b in range(TILE_STEPS):
            s = slice(b * R, (b + 1) * R)
            g, normed = gn[:, s], nrm[:, s]
            out = istd[:, s] * (g - jnp.mean(g, axis=0, keepdims=True)
                                - normed * jnp.mean(g * normed, axis=0, keepdims=True))
            ge[:, pl.ds(own + base + b * R, R)] = out.astype(jnp.bfloat16)

        @pl.when(tile == PAIRS // 2 - 1)
        def _():
            ge_left.start()

        @pl.when(tile == PAIRS - 1)
        def _():
            ge_right.start()

        branch = jnp.dot(woutt[...], act[:, here], preferred_element_type=jnp.float32).astype(jnp.bfloat16)
        bo = (xe[:, pl.ds(own + base, TILE)].astype(jnp.float32) + branch.astype(jnp.float32)).astype(jnp.bfloat16)
        for j in range(J):
            bs[j, :, here] = bo[j * cl:(j + 1) * cl]
        for c in tile_sends(bs, br, bo_base, tile):
            c.start()
        return carry

    lax.fori_loop(0, PAIRS, tile_body, 0)

    def term_body(zz, carry):
        cols = pl.ds(pl.multiple_of(zz * 256, 256), 256)
        both = jnp.concatenate([ctf[j] for j in range(J)], axis=0)
        for i, (a, b) in enumerate(((nb[...], gp), (both, act))):
            term = lax.dot_general(a, b[cols, :], (((1,), (1,)), ((), ())),
                                   preferred_element_type=jnp.float32) * grad_scale
            for h in range(2):
                part = term[:, h * 128:(h + 1) * 128]
                gfull[h, zz, i] = part
                gsend[h, zz, i] = part.astype(jnp.bfloat16)
        rcopy(gsend.at[1 - core, zz], grecv.at[zz], core_base + zz, z * 2 + 1 - core, me_j).start()
        return carry

    lax.fori_loop(0, Z, term_body, 0)

    for j in range(J):
        ch = slice(j * cl, (j + 1) * cl)
        sums = []
        for t in range(TAPS):
            acc = jnp.zeros((cl, R), jnp.float32)
            for k in range(K):
                acc = acc + (ge[ch, own + k * R:own + (k + 1) * R].astype(jnp.float32)
                             * xe[ch, (k + t) * R:(k + t + 1) * R].astype(jnp.float32))
            sums.append(jnp.sum(acc, axis=1, keepdims=True) * grad_scale)
        kp[j] = jnp.concatenate(sums + [jnp.zeros((cl, 128 - TAPS), jnp.float32)], axis=1)
    k_in = to_chan(kp, kr)

    ge_left.wait_recv()
    ge_right.wait_recv()
    pending.extend([ge_left, ge_right])

    def back_body(tile, carry):
        base = pl.multiple_of(tile * TILE, TILE)
        for h in range(TILE_STEPS):
            off = base + h * R
            for j in range(J):
                ch = slice(j * cl, (j + 1) * cl)
                acc = ctf[j, :, pl.ds(off, R)].astype(jnp.float32)
                for t in range(TAPS):
                    acc = acc + tf[t, ch, :] * ge[ch, pl.ds(off + (TAPS - 1 - t) * R, R)].astype(jnp.float32)
                gs[j, :, pl.ds(off, R)] = acc.astype(jnp.bfloat16)
        for c in tile_sends(gs, gr, gs_base, tile):
            c.start()
        return carry

    lax.fori_loop(0, PAIRS, back_body, 0)

    CR = C // J

    def core_sum(zz, carry):
        c = rcopy(gsend.at[1 - core, zz], grecv.at[zz], core_base + zz, z * 2 + 1 - core, me_j)
        c.wait_recv()
        c.wait_send()
        for i in range(2):
            h = gfull[core, zz, i] + grecv[zz, i].astype(jnp.float32)
            for j in range(J):
                hf[j, zz, i] = h[j * CR:(j + 1) * CR]
                hs[j, zz, i] = h[j * CR:(j + 1) * CR].astype(jnp.bfloat16)
        return carry

    lax.fori_loop(0, Z, core_sum, 0)
    h_in = to_chan(hs, hr)
    for c in k_in:
        c.wait_recv()
    total = kp[me_j]
    for d in range(1, J):
        total = total + kr[lax.rem(me_j + J - d, J)]
    kt[me_l] = total
    kt_in = []
    for l in loop_peers:
        c = rcopy(kt.at[me_l], kt.at[me_l], take(), l, me_j)
        c.start()
        kt_in.append(c)
    pending.extend(kt_in)

    def finish(src, buf, base, out):
        buf[me_j] = src[me_j]
        for tile in range(PAIRS):
            for c in tile_sends(src, buf, base, tile):
                c.wait_recv()
                c.wait_send()
        for s in range(J):
            for k in range(K):
                at = k * DILATION_STEP + s * R
                out[:, at:at + R] = buf[s, :, k * R:(k + 1) * R]

    finish(bs, br, bo_base, bo_out)
    for c in h_in:
        c.wait_recv()
    for zz in range(Z):
        total = hf[me_j, zz]
        for d in range(1, J):
            total = total + hr[lax.rem(me_j + J - d, J), zz].astype(jnp.float32)
        sf[zz] = total
    z_in = []
    for e in range(1, Z):
        zz = lax.rem(z + e, Z)
        c = rcopy(sf.at[zz], tr.at[z], take(), zz * 2 + core, me_j)
        c.start()
        z_in.append(c)
    pending.extend(z_in)
    finish(gs, gr, gs_base, gx_out)
    for c in kt_in:
        c.wait_recv()
    total = kt[0]
    for l in range(1, L):
        total = total + kt[l]
    gk_out[...] = total.T[0:TAPS, :]
    for c in z_in:
        c.wait_recv()
    total = sf[z]
    for e in range(1, Z):
        total = total + tr[lax.rem(z + Z - e, Z)]
    gw_in_out[...] = total[0]
    gw_out_out[...] = total[1]
    for c in pending:
        c.wait_send()


def fits(L, J, rows, cl, F):
    R = DILATION_STEP // J
    return (cl * 2 == 128 and rows == 2 * MIDDLE * DILATION_STEP and L % 2 == 0 and L > 2 and J > 1
            and F == L * 128 and R == 128)


def fused_shards(features, kernel_tap_rows, in_weight, out_weight, cotangent):
    L, J = lax.axis_size("loop"), lax.axis_size("chan")
    rows, cl = features.shape
    C, F = in_weight.shape
    if not fits(L, J, rows, cl, F):
        return shards(features, kernel_tap_rows, in_weight, out_weight, cotangent)
    R = DILATION_STEP // J
    K = rows // DILATION_STEP
    N = K * R
    Z = L // 2
    CR = C // J
    bf, f32 = jnp.bfloat16, jnp.float32
    ext = N + 2 * MIDDLE * R
    packed = pltpu.VMEM((J, cl, N), bf)
    scratch = [
        pltpu.VMEM((J, 16, 128), f32),
        pltpu.VMEM((TAPS, C, R), f32),
        pltpu.VMEM((F, C), bf),
        pltpu.VMEM((C, F), bf),
        packed,
        pltpu.VMEM((C, ext), bf),
        packed, packed, packed,
        pltpu.VMEM((C, N), bf),
        pltpu.VMEM((C, 2 * R), f32),
        pltpu.VMEM((1, 2 * R), f32),
        pltpu.VMEM((F, N), bf),
        pltpu.VMEM((F, N), bf),
        pltpu.VMEM((C, ext), bf),
        packed, packed,
        packed, packed,
        pltpu.VMEM((2, Z, 2, C, 128), f32),
        pltpu.VMEM((2, Z, 2, C, 128), bf),
        pltpu.VMEM((Z, 2, C, 128), bf),
        pltpu.VMEM((J, Z, 2, CR, 128), f32),
        pltpu.VMEM((J, Z, 2, CR, 128), bf),
        pltpu.VMEM((J, Z, 2, CR, 128), bf),
        pltpu.VMEM((Z, 2, CR, 128), f32),
        pltpu.VMEM((Z, 2, CR, 128), f32),
        pltpu.VMEM((J, cl, 128), f32),
        pltpu.VMEM((J, cl, 128), f32),
        pltpu.VMEM((L, cl, 128), f32),
    ]
    copies = (J - 1) * 5 + 4 + 2 * (K // 2) * (J - 1) + Z + (L - 1) + (Z - 1)
    scratch += [pltpu.SemaphoreType.DMA((copies,)), pltpu.SemaphoreType.DMA((copies,))]
    vmem = pl.BlockSpec(memory_space=pltpu.VMEM)
    bo, gx, gw_in, gw_out, gk = pl.pallas_call(
        functools.partial(fused_kernel, L, J, 1.0 / math.sqrt(rows * L)),
        out_shape=(
            jax.ShapeDtypeStruct((cl, rows), bf),
            jax.ShapeDtypeStruct((cl, rows), bf),
            jax.ShapeDtypeStruct((CR, F // L), f32),
            jax.ShapeDtypeStruct((CR, F // L), f32),
            jax.ShapeDtypeStruct((TAPS, cl), f32),
        ),
        in_specs=[vmem] * 5,
        out_specs=(vmem,) * 5,
        scratch_shapes=scratch,
        compiler_params=pltpu.CompilerParams(
            collective_id=0, has_side_effects=True, vmem_limit_bytes=50 * 1024 * 1024),
        cost_estimate=pl.CostEstimate(flops=12 * N * C * F, bytes_accessed=8 * rows * cl * 2, transcendentals=N * F),
    )(features.T, cotangent.T, kernel_tap_rows, in_weight, out_weight)
    return bo.T, gx.T, gw_in, gw_out.T, gk


def solution(mesh):
    placed = (P("loop", "chan"), P(None, "chan"), P(), P(), P("loop", "chan"))
    return jax.shard_map(
        fused_shards,
        mesh=mesh,
        in_specs=placed,
        out_specs=(
            P("loop", "chan"),
            P("loop", "chan"),
            P("chan", "loop"),
            P("loop", "chan"),
            P(None, "chan"),
        ),
        check_vma=False,
    )
```

profile of v0, /device:TPU:0, one launch (start us, length us, event | category | flops | bytes accessed | tf_op | source)
XLA Modules:
  0.0 61.4 jit_solution(881725201988759851)
XLA Ops:
  0.6 0.0 copy-start
  0.6 1.0 %copy-done = bf16[4096,64]{0,1:T(8,128)(2,1)S(1)} copy-done((bf16[4096,64]{0,1:T(8,128)(2,1)S(1)}, bf16[4096,64]{0,1:T(8,128)(2,1)}, u32[]{:S(2)}) %copy-start) | copy-done | bytes 524312
  1.7 0.0 copy-start.1
  1.7 1.0 %copy-done.1 = bf16[4096,64]{0,1:T(8,128)(2,1)S(1)} copy-done((bf16[4096,64]{0,1:T(8,128)(2,1)S(1)}, bf16[4096,64]{0,1:T(8,128)(2,1)}, u32[]{:S(2)}) %copy-start.1) | copy-done | bytes 524312
  2.7 0.0 copy-start.2
  2.7 1.0 %copy-done.2 = bf16[256,1024]{1,0:T(8,128)(2,1)S(1)} copy-done((bf16[256,1024]{1,0:T(8,128)(2,1)S(1)}, bf16[256,1024]{1,0:T(8,128)(2,1)}, u32[]{:S(2)}) %copy-start.2) | copy-done | bytes 524312
  3.8 0.0 copy-start.3
  3.8 1.0 %copy-done.3 = bf16[1024,256]{1,0:T(8,128)(2,1)S(1)} copy-done((bf16[1024,256]{1,0:T(8,128)(2,1)S(1)}, bf16[1024,256]{1,0:T(8,128)(2,1)}, u32[]{:S(2)}) %copy-start.3) | copy-done | bytes 524312
  4.8 0.0 copy-start.4
  4.8 0.7 %copy-done.4 = f32[9,64]{1,0:T(8,128)S(1)} copy-done((f32[9,64]{1,0:T(8,128)S(1)}, f32[9,64]{1,0:T(8,128)}, u32[]{:S(2)}) %copy-start.4) | copy-done | bytes 2328
  5.5 52.5 %shard_map.92 = (bf16[64,4096]{1,0:T(8,128)(2,1)S(1)}, bf16[64,4096]{1,0:T(8,128)(2,1)S(1)}, f32[64,128]{1,0:T(8,128)S(1)}, f32[64,128]{1,0:T(8,128)S(1)}, f32[9,64]{1,0:T(8,128)S(1)}) custom-call(bf16[64,4096]{1,0:T(8,128)(2,1)S(1)} %bitcast.8, bf16[64,4096]{1,0:T(8,128)(2,1)S(1)} %bitcast.9, f32[9,64]{1,0:T(8,128)S(1)} %copy-done.4, ...), custom_call_target="tpu_custom_call" | custom-call | flops 3221225472 | bytes 4194304 | tf_op jit(solution)/shard_map/pallas_call | solution.py:494
  58.0 0.8 %copy.15 = bf16[4096,64]{0,1:T(8,128)(2,1)} copy(bf16[4096,64]{0,1:T(8,128)(2,1)S(1)} %bitcast.6) | data formatting | bytes 1048576
  58.8 0.8 %copy.16 = bf16[4096,64]{0,1:T(8,128)(2,1)} copy(bf16[4096,64]{0,1:T(8,128)(2,1)S(1)} %bitcast.5) | data formatting | bytes 1048576
  59.6 0.6 copy.17
  60.2 0.6 copy.18
  60.8 0.6 copy.19
Async XLA Ops:
  0.6 1.0 %copy-start = (bf16[4096,64]{0,1:T(8,128)(2,1)S(1)}, bf16[4096,64]{0,1:T(8,128)(2,1)}, u32[]{:S(2)}) copy-start(bf16[4096,64]{0,1:T(8,128)(2,1)} %param.5) | copy-start | bytes 1572868
  1.7 1.0 %copy-start.1 = (bf16[4096,64]{0,1:T(8,128)(2,1)S(1)}, bf16[4096,64]{0,1:T(8,128)(2,1)}, u32[]{:S(2)}) copy-start(bf16[4096,64]{0,1:T(8,128)(2,1)} %param.9) | copy-start | bytes 1572868
  2.7 1.0 %copy-start.2 = (bf16[256,1024]{1,0:T(8,128)(2,1)S(1)}, bf16[256,1024]{1,0:T(8,128)(2,1)}, u32[]{:S(2)}) copy-start(bf16[256,1024]{1,0:T(8,128)(2,1)} %win.1) | copy-start | bytes 1572868
  3.8 1.0 %copy-start.3 = (bf16[1024,256]{1,0:T(8,128)(2,1)S(1)}, bf16[1024,256]{1,0:T(8,128)(2,1)}, u32[]{:S(2)}) copy-start(bf16[1024,256]{1,0:T(8,128)(2,1)} %wout.1) | copy-start | bytes 1572868
  4.8 0.7 %copy-start.4 = (f32[9,64]{1,0:T(8,128)S(1)}, f32[9,64]{1,0:T(8,128)}, u32[]{:S(2)}) copy-start(f32[9,64]{1,0:T(8,128)} %taps.1) | copy-start | bytes 6916
where the time goes:
time: 61.8 us; the launch traced here: 61.4 us
  Pallas kernels  52.5 us (85%)
  local copies, waits for them, and re-layouts  8.27 us (13%)
  between operations  0.66 us (1%)
    pallas_call x1, Pallas kernels, fused_shards(): pl.pallas_call(functools.partial(fused_kernel, L, J, 1.0 / math.sqrt(rows...  52.5 us
    unnamed x15, local copies, waits for them, and re-layouts  8.27 us

commit v1 on v0

v1 whole, which is shorter than its diff:
```python
import functools
import math

import jax
import jax.numpy as jnp
from jax import lax
from jax.experimental import pallas as pl
from jax.experimental.pallas import tpu as pltpu
from jax.sharding import PartitionSpec as P

TAPS = 9
DILATION_STEP = 512


gelu_scale = math.sqrt(2.0 / math.pi)
cubic_coef = 0.044715
epsilon = 1e-05


def with_halo(cells, sides, width):
    for axis, dim in sides:
        count = lax.axis_size(axis)
        head = lax.slice_in_dim(cells, 0, width, axis=dim)
        tail = lax.slice_in_dim(cells, cells.shape[dim] - width, cells.shape[dim], axis=dim)
        cells = jnp.concatenate(
            [
                lax.ppermute(tail, axis, [(i, (i + 1) % count) for i in range(count)]),
                cells,
                lax.ppermute(head, axis, [((i + 1) % count, i) for i in range(count)]),
            ],
            axis=dim,
        )
    return cells


def gelu_pair(inputs):
    inner_arg = gelu_scale * (inputs + cubic_coef * inputs * inputs * inputs)
    tangent = jnp.tanh(inner_arg)
    act_value = 0.5 * inputs * (1.0 + tangent)
    act_slope = 0.5 * (1.0 + tangent) + 0.5 * inputs * (1.0 - tangent * tangent) * gelu_scale * (
        1.0 + 3.0 * cubic_coef * inputs * inputs
    )
    return (act_value, act_slope)


def widen_rows(field_rows, reach_positions):
    return with_halo(field_rows, (("loop", 0),), reach_positions)


def shards(features, kernel_tap_rows, in_weight, out_weight, cotangent):
    middle_position = (TAPS - 1) // 2
    reach_positions = middle_position * DILATION_STEP
    loop_size = lax.axis_size("loop")
    chan_size = lax.axis_size("chan")
    rows_here = features.shape[0]
    grad_scale = 1.0 / math.sqrt(rows_here * loop_size)
    padded_in = widen_rows(features, reach_positions)
    blended_sum = jnp.zeros(features.shape, jnp.float32)
    for kernel_tap_index in range(TAPS):
        leading_row = reach_positions + (kernel_tap_index - middle_position) * DILATION_STEP
        blended_sum = blended_sum + kernel_tap_rows[kernel_tap_index] * padded_in[
            leading_row : leading_row + rows_here
        ].astype(jnp.float32)
    filtered = blended_sum.astype(jnp.bfloat16)
    row_block, upstream = (
        lax.all_to_all(filtered, "chan", split_axis=0, concat_axis=1, tiled=True),
        lax.all_to_all(cotangent, "chan", split_axis=0, concat_axis=1, tiled=True),
    )
    values = row_block.astype(jnp.float32)
    mean_value = jnp.mean(values, axis=-1, keepdims=True)
    centred = values - mean_value
    variance = jnp.mean(centred * centred, axis=-1, keepdims=True)
    inv_std = lax.rsqrt(variance + epsilon)
    normed = centred * inv_std
    normed_b = normed.astype(jnp.bfloat16)
    hidden_pre = jnp.dot(normed_b, in_weight, preferred_element_type=jnp.float32)
    act_value, act_slope = gelu_pair(hidden_pre)
    act_b = act_value.astype(jnp.bfloat16)
    branch = jnp.dot(act_b, out_weight, preferred_element_type=jnp.float32).astype(jnp.bfloat16)
    grad_act = jnp.einsum("pc,fc->pf", upstream, out_weight, preferred_element_type=jnp.float32)
    grad_pre = (grad_act * act_slope).astype(jnp.bfloat16)
    grad_normed = jnp.einsum("pf,cf->pc", grad_pre, in_weight, preferred_element_type=jnp.float32)
    grad_filtered = inv_std * (
        grad_normed
        - jnp.mean(grad_normed, axis=-1, keepdims=True)
        - normed * jnp.mean(grad_normed * normed, axis=-1, keepdims=True)
    )
    back_rows = grad_filtered.astype(jnp.bfloat16)
    local_rows = row_block.shape[0]
    width_c = row_block.shape[1]
    width_f = hidden_pre.shape[1]
    chan_part = width_c // chan_size
    loop_part = width_f // loop_size
    normed_parts = normed_b.reshape(local_rows, chan_size, chan_part)
    upstream_parts = upstream.reshape(local_rows, chan_size, chan_part)
    grad_parts = grad_pre.reshape(local_rows, loop_size, loop_part)
    act_parts = act_b.reshape(local_rows, loop_size, loop_part)
    term_in = (
        jnp.einsum("pai,pbj->baij", normed_parts, grad_parts, preferred_element_type=jnp.float32)
        * grad_scale
    )
    term_out = (
        jnp.einsum("pbj,pai->baji", act_parts, upstream_parts, preferred_element_type=jnp.float32)
        * grad_scale
    )
    branch_cols, back_cols = (
        lax.all_to_all(branch, "chan", split_axis=1, concat_axis=0, tiled=True),
        lax.all_to_all(back_rows, "chan", split_axis=1, concat_axis=0, tiled=True),
    )
    block_out = (features.astype(jnp.float32) + branch_cols.astype(jnp.float32)).astype(
        jnp.bfloat16
    )
    first_in, first_out = (
        lax.psum_scatter(
            term_in.astype(jnp.bfloat16), "chan", scatter_dimension=1, tiled=True
        ).astype(jnp.float32),
        lax.psum_scatter(
            term_out.astype(jnp.bfloat16), "chan", scatter_dimension=1, tiled=True
        ).astype(jnp.float32),
    )
    summed_in, summed_out = (
        lax.psum_scatter(first_in, "loop", scatter_dimension=0, tiled=True),
        lax.psum_scatter(first_out, "loop", scatter_dimension=0, tiled=True),
    )
    grad_in_weight = summed_in.reshape(chan_part, loop_part)
    grad_out_weight = summed_out.reshape(loop_part, chan_part)
    padded_back = widen_rows(back_cols, reach_positions)
    grad_sum_rows = cotangent.astype(jnp.float32)
    back_wide = back_cols.astype(jnp.float32)
    kernel_rows = []
    for kernel_tap_index in range(TAPS):
        shift_positions = (kernel_tap_index - middle_position) * DILATION_STEP
        first_back = reach_positions - shift_positions
        grad_sum_rows = grad_sum_rows + kernel_tap_rows[kernel_tap_index] * padded_back[
            first_back : first_back + rows_here
        ].astype(jnp.float32)
        first_in_row = reach_positions + shift_positions
        kernel_rows.append(
            jnp.sum(
                back_wide * padded_in[first_in_row : first_in_row + rows_here].astype(jnp.float32),
                axis=0,
            )
        )
    kernel_terms = jnp.stack(kernel_rows) * grad_scale
    grad_kernel = lax.psum(kernel_terms, "loop")
    return (
        block_out,
        grad_sum_rows.astype(jnp.bfloat16),
        grad_in_weight,
        grad_out_weight,
        grad_kernel,
    )


MESH = pl.DeviceIdType.MESH
MIDDLE = (TAPS - 1) // 2
HBM = pltpu.MemorySpace.HBM


def fused_kernel(
    L, J, grad_scale,
    x_hbm, ct_hbm, taps_hbm, win_hbm, wout_hbm,
    bo_out, gx_out, gw_in_out, gw_out_out, gk_out,
    xp, ctv, tapv, win, wout, wint, woutt, tf, fb, fr, ctf, nb, nrm, istd, act, gp,
    geb, brb, gep, brv, gfull, gsend, grecv, hf, hs, hr, sf, sb, tr, gka, kt,
    load, send, recv,
):
    cl, rows = ctv.shape
    C, F = win.shape
    B = DILATION_STEP
    K = rows // B
    S = K // 2
    W = 2 * B // J
    Z = L // 2
    own = MIDDLE * B
    bf, f32 = jnp.bfloat16, jnp.float32
    me_l, me_j = lax.axis_index("loop"), lax.axis_index("chan")
    core, z = lax.rem(me_l, 2), me_l // 2
    used = [0]

    def take(n=1):
        used[0] += n
        return used[0] - n

    def rcopy(src, dst, idx, l, j):
        return pltpu.make_async_remote_copy(
            src_ref=src, dst_ref=dst, send_sem=send.at[idx], recv_sem=recv.at[idx],
            device_id=(l, j), device_id_type=MESH)

    def lanes(at, n):
        return pl.ds(pl.multiple_of(at, 128), n)

    loads = [pltpu.make_async_copy(a, b, load.at[i]) for i, (a, b) in enumerate((
        (x_hbm, xp.at[:, own:own + rows]), (ct_hbm, ctv), (taps_hbm, tapv), (win_hbm, win), (wout_hbm, wout)))]
    for c in loads:
        c.start()

    chan_peers = [lax.rem(me_j + d, J) for d in range(1, J)]
    loop_peers = [lax.rem(me_l + e, L) for e in range(1, L)]
    right, left = loop_peers[0], loop_peers[-1]

    barrier = pltpu.get_barrier_semaphore()
    for j in chan_peers:
        pl.semaphore_signal(barrier, inc=1, device_id=(me_l, j), device_id_type=MESH)
    for l in loop_peers:
        pl.semaphore_signal(barrier, inc=1, device_id=(l, me_j), device_id_type=MESH)

    half = J // 2
    mine = pl.ds(pl.multiple_of(me_j * cl, cl), cl)

    def col(s, j):
        return lanes((S - 1 - s + (j // half) * (1 + 2 * s)) * B + lax.rem(j, half) * W, W)

    def own_col(s, j):
        return lanes(own + (S - 1 - s + (j // half) * (1 + 2 * s)) * B + lax.rem(j, half) * W, W)

    def block(k):
        return lanes(k * B, B)

    def chan_rows(j):
        return pl.ds(pl.multiple_of(j * cl, cl), cl)

    ct_base, f_base = take(S * (J - 1)), take(S * (J - 1))
    ge_base, br_base = take(S * (J - 1)), take(S * (J - 1))
    xh_base, gh_base = take(S * 2), take(S * 2)
    core_base = take(Z)

    def ct_copies(s):
        return [rcopy(ctv.at[:, col(s, j)], ctf.at[s, mine, :], ct_base + s * (J - 1) + d, me_l, j)
                for d, j in enumerate(chan_peers)]

    def f_copies(s):
        return [rcopy(fb.at[:, col(s, j)], fr.at[s, mine, :], f_base + s * (J - 1) + d, me_l, j)
                for d, j in enumerate(chan_peers)]

    def ge_copies(s):
        return [rcopy(geb.at[s, chan_rows(j), :], gep.at[:, own_col(s, me_j)], ge_base + s * (J - 1) + d, me_l, j)
                for d, j in enumerate(chan_peers)]

    def br_copies(s):
        return [rcopy(brb.at[s, chan_rows(j), :], brv.at[:, col(s, me_j)], br_base + s * (J - 1) + d, me_l, j)
                for d, j in enumerate(chan_peers)]

    def halo_copies(buf, right_block, left_block, base):
        return [rcopy(buf.at[:, block(right_block + S)], buf.at[:, block(right_block - S)], base, right, me_j),
                rcopy(buf.at[:, block(left_block + S)], buf.at[:, block(left_block + K + S)], base + 1, left, me_j)]

    def xh_copies(s):
        return halo_copies(xp, K - 1 - s, s, xh_base + 2 * s)

    def gh_copies(s):
        return halo_copies(gep, S + s, S - 1 - s, gh_base + 2 * s)

    def start(copies):
        for c in copies:
            c.start()

    def arrive(copies):
        for c in copies:
            c.wait_recv()

    loads[0].wait()
    loads[1].wait()
    pl.semaphore_wait(barrier, J - 1 + L - 1)
    for s in range(S):
        start(xh_copies(s))
    for s in range(S - 1):
        start(ct_copies(s))

    for c in loads[2:]:
        c.wait()
    padded = jnp.concatenate([tapv[...], jnp.zeros((128 - TAPS, cl), f32)], axis=0)
    columns = jnp.concatenate([padded, jnp.zeros((128, 128 - cl), f32)], axis=1).T
    for t in range(TAPS):
        tf[t] = jnp.broadcast_to(columns[0:cl, t:t + 1], (cl, 128))
    wint[...] = win[...].T
    woutt[...] = wout[...].T
    gka[...] = jnp.zeros(gka.shape, f32)
    for s in range(S):
        ctf[s, mine, :] = ctv[:, col(s, me_j)]

    def conv_body(s, carry):
        arrive(xh_copies(s))
        for g in range(cl // 16):
            ch = slice(g * 16, (g + 1) * 16)
            w = [tf[t, ch, :] for t in range(TAPS)]
            for k in (S - 1 - s, S + s):
                for q in range(B // 128):
                    acc = jnp.zeros((16, 128), f32)
                    for t in range(TAPS):
                        acc = acc + w[t] * xp[ch, lanes((k + t) * B + q * 128, 128)].astype(f32)
                    fb[ch, lanes(k * B + q * 128, 128)] = acc.astype(bf)
        start(f_copies(s))
        fr[s, mine, :] = fb[:, col(s, me_j)]

        @pl.when(s == 0)
        def _():
            start(ct_copies(S - 1))
        return carry

    lax.fori_loop(0, S, conv_body, 0)

    def mlp_body(s, carry):
        arrive(ct_copies(s))
        arrive(f_copies(s))
        here = lanes(s * W, W)
        for b in range(W // 128):
            part = slice(b * 128, (b + 1) * 128)
            v = fr[s, :, part].astype(f32)
            centred = v - jnp.mean(v, axis=0, keepdims=True)
            inv = lax.rsqrt(jnp.mean(centred * centred, axis=0, keepdims=True) + epsilon)
            normed = centred * inv
            nrm[:, part] = normed
            istd[:, part] = inv
            nb[:, lanes(s * W + b * 128, 128)] = normed.astype(bf)
        normed_b = nb[:, here]
        up = ctf[s]
        FC = 256
        for f in range(F // FC):
            part = slice(f * FC, (f + 1) * FC)
            pre = jnp.dot(wint[part, :], normed_b, preferred_element_type=f32)
            ga = jnp.dot(wout[part, :], up, preferred_element_type=f32)
            sq = pre * pre
            tangent = jnp.tanh(pre * (gelu_scale + (gelu_scale * cubic_coef) * sq))
            gate = 0.5 + 0.5 * tangent
            slope = gate + pre * (gate * (1.0 - tangent)) * (gelu_scale + (3.0 * gelu_scale * cubic_coef) * sq)
            act[part, here] = (pre * gate).astype(bf)
            gp[part, here] = (ga * slope).astype(bf)
        gn = jnp.dot(win[...], gp[:, here], preferred_element_type=f32)
        for b in range(W // 128):
            part = slice(b * 128, (b + 1) * 128)
            g, normed = gn[:, part], nrm[:, part]
            out = istd[:, part] * (g - jnp.mean(g, axis=0, keepdims=True)
                                   - normed * jnp.mean(g * normed, axis=0, keepdims=True))
            geb[s, :, part] = out.astype(bf)
        start(ge_copies(s))
        gep[:, own_col(s, me_j)] = geb[s, mine, :]
        brb[s] = jnp.dot(woutt[...], act[:, here], preferred_element_type=f32).astype(bf)
        brv[:, col(s, me_j)] = brb[s, mine, :]

        @pl.when(s == 1)
        def _():
            start(br_copies(0))
        return carry

    lax.fori_loop(0, S, mlp_body, 0)

    def forward(s):
        arrive(ge_copies(s))
        start(gh_copies(s))

    def kernel_terms(s):
        for g in range(cl // 16):
            ch = slice(g * 16, (g + 1) * 16)
            sums = [gka[t, ch, :] for t in range(TAPS)]
            for k in (S - 1 - s, S + s):
                for q in range(B // 128):
                    e = gep[ch, lanes(own + k * B + q * 128, 128)].astype(f32)
                    for t in range(TAPS):
                        sums[t] = sums[t] + e * xp[ch, lanes((k + t) * B + q * 128, 128)].astype(f32)
            for t in range(TAPS):
                gka[t, ch, :] = sums[t]

    forward(0)

    def term_body(zz, carry):
        cols = lanes(zz * 256, 256)
        both = jnp.concatenate([ctf[s] for s in range(S)], axis=1)
        for i, (a, b) in enumerate(((nb[...], gp), (both, act))):
            term = lax.dot_general(a, b[cols, :], (((1,), (1,)), ((), ())), preferred_element_type=f32) * grad_scale
            for h in range(2):
                part = term[:, h * 128:(h + 1) * 128]
                gfull[h, zz, i] = part
                gsend[h, zz, i] = part.astype(bf)
        rcopy(gsend.at[1 - core, zz], grecv.at[zz], core_base + zz, z * 2 + 1 - core, me_j).start()
        return carry

    lax.fori_loop(0, Z, term_body, 0)
    forward(1)
    start(br_copies(1))

    CR = C // J

    def core_sum(zz, carry):
        c = rcopy(gsend.at[1 - core, zz], grecv.at[zz], core_base + zz, z * 2 + 1 - core, me_j)
        c.wait_recv()
        c.wait_send()
        for i in range(2):
            h = gfull[core, zz, i] + grecv[zz, i].astype(f32)
            for j in range(J):
                hf[j, zz, i] = h[j * CR:(j + 1) * CR]
                hs[j, zz, i] = h[j * CR:(j + 1) * CR].astype(bf)
        return carry

    lax.fori_loop(0, Z, core_sum, 0)
    h_in = [rcopy(hs.at[j], hr.at[me_j], take(), me_l, j) for j in chan_peers]
    start(h_in)
    start(br_copies(2))
    start(br_copies(3))

    def early_terms(s, carry):
        kernel_terms(s)
        return carry

    def late_terms(s, carry):
        forward(s)
        kernel_terms(s)
        return carry

    lax.fori_loop(0, 2, early_terms, 0)
    lax.fori_loop(2, S, late_terms, 0)
    sums = [jnp.sum(gka[t], axis=1, keepdims=True) * grad_scale for t in range(TAPS)]
    total = jnp.concatenate(sums + [jnp.zeros((cl, 128 - TAPS), f32)], axis=1)
    total = jnp.concatenate([total, jnp.zeros((128 - cl, 128), f32)], axis=0).T
    kt[me_l] = total[0:16]
    kt_in = [rcopy(kt.at[me_l], kt.at[me_l], take(), l, me_j) for l in loop_peers]
    start(kt_in)

    for s in range(S):
        arrive(gh_copies(s))

    def back_body(k, carry):
        for g in range(cl // 16):
            ch = slice(g * 16, (g + 1) * 16)
            w = [tf[t, ch, :] for t in range(TAPS)]
            for q in range(B // 128):
                at = lanes(k * B + q * 128, 128)
                acc = ctv[ch, at].astype(f32)
                for t in range(TAPS):
                    acc = acc + w[t] * gep[ch, lanes((k + TAPS - 1 - t) * B + q * 128, 128)].astype(f32)
                gx_out[ch, at] = acc.astype(bf)
        return carry

    lax.fori_loop(0, K, back_body, 0)

    arrive(h_in)
    for zz in range(Z):
        total = hf[me_j, zz]
        for d in range(1, J):
            total = total + hr[lax.rem(me_j + J - d, J), zz].astype(f32)
        sf[zz] = total
        sb[zz] = total.astype(bf)
    z_in = []
    for e in range(1, Z):
        zz = lax.rem(z + e, Z)
        z_in.append(rcopy(sb.at[zz], tr.at[z], take(), zz * 2 + core, me_j))
    start(z_in)

    def finish(s, carry):
        arrive(br_copies(s))
        for k in (S - 1 - s, S + s):
            bo_out[:, block(k)] = (xp[:, block(k + S)].astype(f32) + brv[:, block(k)].astype(f32)).astype(bf)
        return carry

    lax.fori_loop(0, S, finish, 0)
    arrive(kt_in)
    total = kt[0]
    for l in range(1, L):
        total = total + kt[l]
    gk_out[...] = total[0:TAPS, 0:cl]
    arrive(z_in)
    total = sf[z]
    for e in range(1, Z):
        total = total + tr[lax.rem(z + Z - e, Z)].astype(f32)
    gw_in_out[...] = total[0]
    gw_out_out[...] = total[1]

    def sent(s, carry):
        for copies in (ct_copies(s), f_copies(s), ge_copies(s), br_copies(s), xh_copies(s), gh_copies(s)):
            for c in copies:
                c.wait_send()
        return carry

    lax.fori_loop(0, S, sent, 0)
    for c in h_in + kt_in + z_in:
        c.wait_send()


def flush_kernel(*refs):
    n = len(refs) // 2
    sems = refs[2 * n]
    copies = [pltpu.make_async_copy(refs[i], refs[n + i], sems.at[i]) for i in range(n)]
    for c in copies:
        c.start()
    for c in copies:
        c.wait()


def fits(L, J, rows, cl, F):
    return (cl * 2 == 128 and rows == 2 * MIDDLE * DILATION_STEP and L % 2 == 0 and L > 2 and J == 4
            and F == L * 128)


def fused_shards(features, kernel_tap_rows, in_weight, out_weight, cotangent):
    L, J = lax.axis_size("loop"), lax.axis_size("chan")
    rows, cl = features.shape
    C, F = in_weight.shape
    if not fits(L, J, rows, cl, F):
        return shards(features, kernel_tap_rows, in_weight, out_weight, cotangent)
    N = rows // J
    K = rows // DILATION_STEP
    S = K // 2
    W = N // S
    Z = L // 2
    CR = C // J
    bf, f32 = jnp.bfloat16, jnp.float32
    ext = rows + 2 * MIDDLE * DILATION_STEP
    scratch = [
        pltpu.VMEM((cl, ext), bf),
        pltpu.VMEM((cl, rows), bf),
        pltpu.VMEM((TAPS, cl), f32),
        pltpu.VMEM((C, F), bf),
        pltpu.VMEM((F, C), bf),
        pltpu.VMEM((F, C), bf),
        pltpu.VMEM((C, F), bf),
        pltpu.VMEM((TAPS, cl, 128), f32),
        pltpu.VMEM((cl, rows), bf),
        pltpu.VMEM((S, C, W), bf),
        pltpu.VMEM((S, C, W), bf),
        pltpu.VMEM((C, N), bf),
        pltpu.VMEM((C, W), f32),
        pltpu.VMEM((1, W), f32),
        pltpu.VMEM((F, N), bf),
        pltpu.VMEM((F, N), bf),
        pltpu.VMEM((S, C, W), bf),
        pltpu.VMEM((S, C, W), bf),
        pltpu.VMEM((cl, ext), bf),
        pltpu.VMEM((cl, rows), bf),
        pltpu.VMEM((2, Z, 2, C, 128), f32),
        pltpu.VMEM((2, Z, 2, C, 128), bf),
        pltpu.VMEM((Z, 2, C, 128), bf),
        pltpu.VMEM((J, Z, 2, CR, 128), f32),
        pltpu.VMEM((J, Z, 2, CR, 128), bf),
        pltpu.VMEM((J, Z, 2, CR, 128), bf),
        pltpu.VMEM((Z, 2, CR, 128), f32),
        pltpu.VMEM((Z, 2, CR, 128), bf),
        pltpu.VMEM((Z, 2, CR, 128), bf),
        pltpu.VMEM((TAPS, cl, 128), f32),
        pltpu.VMEM((L, 16, 128), f32),
    ]
    copies = 4 * S * (J - 1) + 4 * S + Z + (J - 1) + (L - 1) + (Z - 1)
    scratch += [pltpu.SemaphoreType.DMA((5,)), pltpu.SemaphoreType.DMA((copies,)), pltpu.SemaphoreType.DMA((copies,))]
    vmem = pl.BlockSpec(memory_space=pltpu.VMEM)
    hbm = pl.BlockSpec(memory_space=HBM)
    shapes = (
        jax.ShapeDtypeStruct((cl, rows), bf),
        jax.ShapeDtypeStruct((cl, rows), bf),
        jax.ShapeDtypeStruct((CR, F // L), f32),
        jax.ShapeDtypeStruct((CR, F // L), f32),
        jax.ShapeDtypeStruct((TAPS, cl), f32),
    )
    results = pl.pallas_call(
        functools.partial(fused_kernel, L, J, 1.0 / math.sqrt(rows * L)),
        out_shape=shapes,
        in_specs=[hbm] * 5,
        out_specs=(vmem,) * 5,
        scratch_shapes=scratch,
        compiler_params=pltpu.CompilerParams(
            collective_id=0, has_side_effects=True, vmem_limit_bytes=62 * 1024 * 1024),
        cost_estimate=pl.CostEstimate(flops=12 * N * C * F, bytes_accessed=8 * rows * cl * 2, transcendentals=N * F),
    )(features.T, cotangent.T, kernel_tap_rows, in_weight, out_weight)
    bo, gx, gw_in, gw_out, gk = pl.pallas_call(
        flush_kernel,
        out_shape=shapes,
        in_specs=[pl.BlockSpec(memory_space=pl.ANY)] * 5,
        out_specs=(hbm,) * 5,
        scratch_shapes=[pltpu.SemaphoreType.DMA((5,))],
    )(*results)
    return bo.T, gx.T, gw_in, gw_out.T, gk


def solution(mesh):
    placed = (P("loop", "chan"), P(None, "chan"), P(), P(), P("loop", "chan"))
    return jax.shard_map(
        fused_shards,
        mesh=mesh,
        in_specs=placed,
        out_specs=(
            P("loop", "chan"),
            P("loop", "chan"),
            P("chan", "loop"),
            P("loop", "chan"),
            P(None, "chan"),
        ),
        check_vma=False,
    )
```

time: 61.8 us -> 76.2 us (1.23)
  Pallas kernels: 52.5 us -> 75.4 us
  local copies, waits for them, and re-layouts: 8.27 us -> 0 us
    pallas_call x0 -> x1, Pallas kernels: none -> 35 us  [fused_shards(): pl.pallas_call(flush_kernel, out_shape=shapes, in_specs=[pl.BlockSpec(mem...]
    pallas_call x1, Pallas kernels: 52.5 us -> 40.4 us  [fused_shards(): pl.pallas_call(functools.partial(fused_kernel, L, J, 1.0 / math.sqrt(rows...]
    unnamed x15 -> x0, local copies, waits for them, and re-layouts: 8.27 us -> none
where the time goes in v1:
time: 76.2 us; the launch traced here: 76 us
  Pallas kernels  75.4 us (99%)
    pallas_call x1, Pallas kernels, fused_shards(): pl.pallas_call(functools.partial(fused_kernel, L, J, 1.0 / math.sqrt(rows...  40.4 us
    pallas_call x1, Pallas kernels, fused_shards(): pl.pallas_call(flush_kernel, out_shape=shapes, in_specs=[pl.BlockSpec(mem...  35 us

profile of v1, /device:TPU:0, one launch (start us, length us, event | category | flops | bytes accessed | tf_op | source)
XLA Modules:
  0.0 76.0 jit_solution(864552399742087405)
XLA Ops:
  0.6 40.4 %shard_map.92 = (bf16[64,4096]{1,0:T(8,128)(2,1)}, bf16[64,4096]{1,0:T(8,128)(2,1)}, f32[64,128]{1,0:T(8,128)}, f32[64,128]{1,0:T(8,128)}, f32[9,64]{1,0:T(8,128)}) custom-call(bf16[64,4096]{1,0:T(8,128)(2,1)} %bitcast.5, bf16[64,4096]{1,0:T(8,128)(2,1)} %bitcast.6, f32[9,64]{1,0:T(8,128)} %taps_hbm.1, bf16[256,1024]{1,0:T(8,128)(2,1)} %win_hbm.1, ...), custom_call_target="tpu_custom_call" | custom-call | flops 3221225472 | bytes 4194304 | tf_op jit(solution)/shard_map/pallas_call | solution.py:552
  41.0 35.0 %shard_map.93 = (bf16[64,4096]{1,0:T(8,128)(2,1)}, bf16[64,4096]{1,0:T(8,128)(2,1)}, f32[64,128]{1,0:T(8,128)}, f32[64,128]{1,0:T(8,128)}, f32[9,64]{1,0:T(8,128)}) custom-call(bf16[64,4096]{1,0:T(8,128)(2,1)} %get-tuple-element.15.refs_0_, bf16[64,4096]{1,0:T(8,128)(2,1)} %get-tuple-element.16.refs_1_, f32[64,128]{1,0:T(8,128)} %get-tuple-element.17.refs_2_, ...), custom_call_target="tpu_custom_call" | custom-call | tf_op jit(solution)/shard_map/pallas_call | solution.py:562

commit v2 on v1

--- a/solution.py
+++ b/solution.py
@@ -556,7 +556,7 @@
         out_specs=(vmem,) * 5,
         scratch_shapes=scratch,
         compiler_params=pltpu.CompilerParams(
-            collective_id=0, has_side_effects=True, vmem_limit_bytes=62 * 1024 * 1024),
+            collective_id=0, has_side_effects=True, vmem_limit_bytes=54000 * 1024),
         cost_estimate=pl.CostEstimate(flops=12 * N * C * F, bytes_accessed=8 * rows * cl * 2, transcendentals=N * F),
     )(features.T, cotangent.T, kernel_tap_rows, in_weight, out_weight)
     bo, gx, gw_in, gw_out, gk = pl.pallas_call(
@@ -565,6 +565,7 @@
         in_specs=[pl.BlockSpec(memory_space=pl.ANY)] * 5,
         out_specs=(hbm,) * 5,
         scratch_shapes=[pltpu.SemaphoreType.DMA((5,))],
+        compiler_params=pltpu.CompilerParams(vmem_limit_bytes=1024 * 1024),
     )(*results)
     return bo.T, gx.T, gw_in, gw_out.T, gk
 

time: 76.2 us -> 41.7 us (0.55)
  Pallas kernels: 75.4 us -> 40.1 us
    pallas_call x1, Pallas kernels: 35 us -> 1.02 us  [fused_shards(): pl.pallas_call(flush_kernel, out_shape=shapes, in_specs=[pl.BlockSpec(mem...]
    pallas_call x1, Pallas kernels: 40.4 us -> 39.1 us  [fused_shards(): pl.pallas_call(functools.partial(fused_kernel, L, J, 1.0 / math.sqrt(rows...]
where the time goes in v2:
time: 41.7 us; the launch traced here: 41.5 us
  Pallas kernels  40.1 us (96%)
  local copies, waits for them, and re-layouts  0.69 us (2%)
  between operations  0.65 us (2%)
    pallas_call x1, Pallas kernels, fused_shards(): pl.pallas_call(functools.partial(fused_kernel, L, J, 1.0 / math.sqrt(rows...  39.1 us
    pallas_call x1, Pallas kernels, fused_shards(): pl.pallas_call(flush_kernel, out_shape=shapes, in_specs=[pl.BlockSpec(mem...  1.02 us

profile of v2, /device:TPU:0, one launch (start us, length us, event | category | flops | bytes accessed | tf_op | source)
XLA Modules:
  0.0 41.5 jit_solution(6504015395595661041)
XLA Ops:
  0.6 0.0 copy-start
  0.6 0.7 %copy-done = f32[9,64]{1,0:T(8,128)S(1)} copy-done((f32[9,64]{1,0:T(8,128)S(1)}, f32[9,64]{1,0:T(8,128)}, u32[]{:S(2)}) %copy-start) | copy-done | bytes 2328
  1.3 39.1 %shard_map.92 = (bf16[64,4096]{1,0:T(8,128)(2,1)S(1)}, bf16[64,4096]{1,0:T(8,128)(2,1)S(1)}, f32[64,128]{1,0:T(8,128)S(1)}, f32[64,128]{1,0:T(8,128)S(1)}, f32[9,64]{1,0:T(8,128)S(1)}) custom-call(bf16[64,4096]{1,0:T(8,128)(2,1)} %bitcast.5, bf16[64,4096]{1,0:T(8,128)(2,1)} %bitcast.6, f32[9,64]{1,0:T(8,128)S(1)} %copy-done, bf16[256,1024]{1,0:T(8,128)(2,1)} %win_hbm.1, ...), custom_call_target="tpu_custom_call" | custom-call | flops 3221225472 | bytes 4194304 | tf_op jit(solution)/shard_map/pallas_call | solution.py:552
  40.4 1.0 %shard_map.93 = (bf16[64,4096]{1,0:T(8,128)(2,1)}, bf16[64,4096]{1,0:T(8,128)(2,1)}, f32[64,128]{1,0:T(8,128)}, f32[64,128]{1,0:T(8,128)}, f32[9,64]{1,0:T(8,128)}) custom-call(bf16[64,4096]{1,0:T(8,128)(2,1)S(1)} %get-tuple-element.15.refs_0_, bf16[64,4096]{1,0:T(8,128)(2,1)S(1)} %get-tuple-element.16.refs_1_, f32[64,128]{1,0:T(8,128)S(1)} %get-tuple-element.17.refs_2_, ...), custom_call_target="tpu_custom_call" | custom-call | tf_op jit(solution)/shard_map/pallas_call | solution.py:562
Async XLA Ops:
  0.6 0.7 %copy-start = (f32[9,64]{1,0:T(8,128)S(1)}, f32[9,64]{1,0:T(8,128)}, u32[]{:S(2)}) copy-start(f32[9,64]{1,0:T(8,128)} %taps_hbm.1) | copy-start | bytes 6916

commit v3 on v2

--- a/solution.py
+++ b/solution.py
@@ -162,7 +162,7 @@
     x_hbm, ct_hbm, taps_hbm, win_hbm, wout_hbm,
     bo_out, gx_out, gw_in_out, gw_out_out, gk_out,
     xp, ctv, tapv, win, wout, wint, woutt, tf, fb, fr, ctf, nb, nrm, istd, act, gp,
-    geb, brb, gep, brv, gfull, gsend, grecv, hf, hs, hr, sf, sb, tr, gka, kt,
+    geb, brb, gep, brv, gfull, gsend, grecv, hf, hs, hr, sf, sb, tr, zs, tz, vf, vs, vr, gka, kt, acc_x,
     load, send, recv,
 ):
     cl, rows = ctv.shape
@@ -224,6 +224,7 @@
     ge_base, br_base = take(S * (J - 1)), take(S * (J - 1))
     xh_base, gh_base = take(S * 2), take(S * 2)
     core_base = take(Z)
+    h_base, tz_base = take(Z * (J - 1)), take(Z - 1)
 
     def ct_copies(s):
         return [rcopy(ctv.at[:, col(s, j)], ctf.at[s, mine, :], ct_base + s * (J - 1) + d, me_l, j)
@@ -338,12 +339,10 @@
         brb[s] = jnp.dot(woutt[...], act[:, here], preferred_element_type=f32).astype(bf)
         brv[:, col(s, me_j)] = brb[s, mine, :]
 
-        @pl.when(s == 1)
-        def _():
-            start(br_copies(0))
         return carry
 
     lax.fori_loop(0, S, mlp_body, 0)
+    start(br_copies(0))
 
     def forward(s):
         arrive(ge_copies(s))
@@ -362,8 +361,13 @@
                 gka[t, ch, :] = sums[t]
 
     forward(0)
-
-    def term_body(zz, carry):
+    CR = C // J
+
+    def core_copy(zz):
+        return rcopy(gsend.at[1 - core, zz], grecv.at[zz], core_base + zz, z * 2 + 1 - core, me_j)
+
+    def term_body(e, carry):
+        zz = lax.rem(z + 1 + e, Z)
         cols = lanes(zz * 256, 256)
         both = jnp.concatenate([ctf[s] for s in range(S)], axis=1)
         for i, (a, b) in enumerate(((nb[...], gp), (both, act))):
@@ -372,43 +376,55 @@
                 part = term[:, h * 128:(h + 1) * 128]
                 gfull[h, zz, i] = part
                 gsend[h, zz, i] = part.astype(bf)
-        rcopy(gsend.at[1 - core, zz], grecv.at[zz], core_base + zz, z * 2 + 1 - core, me_j).start()
+        core_copy(zz).start()
+
+        @pl.when(e == 1)
+        def _():
+            forward(1)
         return carry
 
     lax.fori_loop(0, Z, term_body, 0)
-    forward(1)
-    start(br_copies(1))
-
-    CR = C // J
-
-    def core_sum(zz, carry):
-        c = rcopy(gsend.at[1 - core, zz], grecv.at[zz], core_base + zz, z * 2 + 1 - core, me_j)
-        c.wait_recv()
-        c.wait_send()
-        for i in range(2):
-            h = gfull[core, zz, i] + grecv[zz, i].astype(f32)
-            for j in range(J):
-                hf[j, zz, i] = h[j * CR:(j + 1) * CR]
-                hs[j, zz, i] = h[j * CR:(j + 1) * CR].astype(bf)
+
+    def h_copies(zz):
+        return [rcopy(hs.at[j, zz], hr.at[me_j, zz], h_base + zz * (J - 1) + d, me_l, j)
+                for d, j in enumerate(chan_peers)]
+
+    def zfirst(e):
+        zz = lax.rem(z + 1 + e, Z)
+        return rcopy(zs.at[zz], tz.at[z], tz_base + e, zz * 2 + core, me_j)
+
+    def core_sum(e, carry):
+        zz = lax.rem(z + 1 + e, Z)
+        core_copy(zz).wait_recv()
+        h = gfull[core, zz, 1] + grecv[zz, 1].astype(f32)
+        gfull[core, zz, 1] = h
+        zs[zz] = h.astype(bf)
+
+        @pl.when(e < Z - 1)
+        def _():
+            zfirst(e).start()
+        h = gfull[core, zz, 0] + grecv[zz, 0].astype(f32)
+        for j in range(J):
+            hf[j, zz] = h[j * CR:(j + 1) * CR]
+            hs[j, zz] = h[j * CR:(j + 1) * CR].astype(bf)
+        start(h_copies(zz))
+
+        @pl.when(e == 1)
+        def _():
+            forward(2)
         return carry
 
     lax.fori_loop(0, Z, core_sum, 0)
-    h_in = [rcopy(hs.at[j], hr.at[me_j], take(), me_l, j) for j in chan_peers]
-    start(h_in)
-    start(br_copies(2))
-    start(br_copies(3))
+    for s in range(1, S):
+        start(br_copies(s))
 
     def early_terms(s, carry):
         kernel_terms(s)
         return carry
 
-    def late_terms(s, carry):
-        forward(s)
-        kernel_terms(s)
-        return carry
-
-    lax.fori_loop(0, 2, early_terms, 0)
-    lax.fori_loop(2, S, late_terms, 0)
+    lax.fori_loop(0, S - 1, early_terms, 0)
+    forward(S - 1)
+    kernel_terms(S - 1)
     sums = [jnp.sum(gka[t], axis=1, keepdims=True) * grad_scale for t in range(TAPS)]
     total = jnp.concatenate(sums + [jnp.zeros((cl, 128 - TAPS), f32)], axis=1)
     total = jnp.concatenate([total, jnp.zeros((128 - cl, 128), f32)], axis=0).T
@@ -416,24 +432,36 @@
     kt_in = [rcopy(kt.at[me_l], kt.at[me_l], take(), l, me_j) for l in loop_peers]
     start(kt_in)
 
-    for s in range(S):
+    def back(final):
+        late = (S - 1, S, S + K - 1, S + K)
+
+        def part(q, carry):
+            for g in range(cl // 16):
+                ch = slice(g * 16, (g + 1) * 16)
+                w = [tf[t, ch, :] for t in range(TAPS)]
+                for k in range(K):
+                    at = lanes(k * B + q * 128, 128)
+                    acc = acc_x[ch, at] if final else ctv[ch, at].astype(f32)
+                    for t in range(TAPS):
+                        b = k + TAPS - 1 - t
+                        if (b in late) == final:
+                            acc = acc + w[t] * gep[ch, lanes(b * B + q * 128, 128)].astype(f32)
+                    if final:
+                        gx_out[ch, at] = acc.astype(bf)
+                    else:
+                        acc_x[ch, at] = acc
+            return carry
+
+        lax.fori_loop(0, B // 128, part, 0)
+
+    for s in range(S - 1):
         arrive(gh_copies(s))
-
-    def back_body(k, carry):
-        for g in range(cl // 16):
-            ch = slice(g * 16, (g + 1) * 16)
-            w = [tf[t, ch, :] for t in range(TAPS)]
-            for q in range(B // 128):
-                at = lanes(k * B + q * 128, 128)
-                acc = ctv[ch, at].astype(f32)
-                for t in range(TAPS):
-                    acc = acc + w[t] * gep[ch, lanes((k + TAPS - 1 - t) * B + q * 128, 128)].astype(f32)
-                gx_out[ch, at] = acc.astype(bf)
-        return carry
-
-    lax.fori_loop(0, K, back_body, 0)
-
-    arrive(h_in)
+    back(False)
+    arrive(gh_copies(S - 1))
+    back(True)
+
+    for zz in range(Z):
+        arrive(h_copies(zz))
     for zz in range(Z):
         total = hf[me_j, zz]
         for d in range(1, J):
@@ -445,6 +473,16 @@
         zz = lax.rem(z + e, Z)
         z_in.append(rcopy(sb.at[zz], tr.at[z], take(), zz * 2 + core, me_j))
     start(z_in)
+    for e in range(Z - 1):
+        zfirst(e).wait_recv()
+    total = gfull[core, z, 1]
+    for e in range(1, Z):
+        total = total + tz[lax.rem(z + Z - e, Z)].astype(f32)
+    for j in range(J):
+        vf[j] = total[j * CR:(j + 1) * CR]
+        vs[j] = total[j * CR:(j + 1) * CR].astype(bf)
+    v_in = [rcopy(vs.at[j], vr.at[me_j], take(), me_l, j) for j in chan_peers]
+    start(v_in)
 
     def finish(s, carry):
         arrive(br_copies(s))
@@ -462,8 +500,12 @@
     total = sf[z]
     for e in range(1, Z):
         total = total + tr[lax.rem(z + Z - e, Z)].astype(f32)
-    gw_in_out[...] = total[0]
-    gw_out_out[...] = total[1]
+    gw_in_out[...] = total
+    arrive(v_in)
+    total = vf[me_j]
+    for d in range(1, J):
+        total = total + vr[lax.rem(me_j + J - d, J)].astype(f32)
+    gw_out_out[...] = total
 
     def sent(s, carry):
         for copies in (ct_copies(s), f_copies(s), ge_copies(s), br_copies(s), xh_copies(s), gh_copies(s)):
@@ -472,7 +514,10 @@
         return carry
 
     lax.fori_loop(0, S, sent, 0)
-    for c in h_in + kt_in + z_in:
+    for zz in range(Z):
+        for c in [core_copy(zz)] + h_copies(zz):
+            c.wait_send()
+    for c in kt_in + z_in + v_in + [zfirst(e) for e in range(Z - 1)]:
         c.wait_send()
 
 
@@ -529,16 +574,22 @@
         pltpu.VMEM((2, Z, 2, C, 128), f32),
         pltpu.VMEM((2, Z, 2, C, 128), bf),
         pltpu.VMEM((Z, 2, C, 128), bf),
-        pltpu.VMEM((J, Z, 2, CR, 128), f32),
-        pltpu.VMEM((J, Z, 2, CR, 128), bf),
-        pltpu.VMEM((J, Z, 2, CR, 128), bf),
-        pltpu.VMEM((Z, 2, CR, 128), f32),
-        pltpu.VMEM((Z, 2, CR, 128), bf),
-        pltpu.VMEM((Z, 2, CR, 128), bf),
+        pltpu.VMEM((J, Z, CR, 128), f32),
+        pltpu.VMEM((J, Z, CR, 128), bf),
+        pltpu.VMEM((J, Z, CR, 128), bf),
+        pltpu.VMEM((Z, CR, 128), f32),
+        pltpu.VMEM((Z, CR, 128), bf),
+        pltpu.VMEM((Z, CR, 128), bf),
+        pltpu.VMEM((Z, C, 128), bf),
+        pltpu.VMEM((Z, C, 128), bf),
+        pltpu.VMEM((J, CR, 128), f32),
+        pltpu.VMEM((J, CR, 128), bf),
+        pltpu.VMEM((J, CR, 128), bf),
         pltpu.VMEM((TAPS, cl, 128), f32),
         pltpu.VMEM((L, 16, 128), f32),
+        pltpu.VMEM((cl, rows), f32),
     ]
-    copies = 4 * S * (J - 1) + 4 * S + Z + (J - 1) + (L - 1) + (Z - 1)
+    copies = 4 * S * (J - 1) + 4 * S + Z + (Z + 1) * (J - 1) + (L - 1) + 2 * (Z - 1)
     scratch += [pltpu.SemaphoreType.DMA((5,)), pltpu.SemaphoreType.DMA((copies,)), pltpu.SemaphoreType.DMA((copies,))]
     vmem = pl.BlockSpec(memory_space=pltpu.VMEM)
     hbm = pl.BlockSpec(memory_space=HBM)
@@ -556,9 +607,10 @@
         out_specs=(vmem,) * 5,
         scratch_shapes=scratch,
         compiler_params=pltpu.CompilerParams(
-            collective_id=0, has_side_effects=True, vmem_limit_bytes=54000 * 1024),
+            collective_id=0, has_side_effects=True, vmem_limit_bytes=50 * 1024 * 1024),
         cost_estimate=pl.CostEstimate(flops=12 * N * C * F, bytes_accessed=8 * rows * cl * 2, transcendentals=N * F),
-    )(features.T, cotangent.T, kernel_tap_rows, in_weight, out_weight)
+    )(*[pltpu.with_memory_space_constraint(a, HBM)
+        for a in (features.T, cotangent.T, kernel_tap_rows, in_weight, out_weight)])
     bo, gx, gw_in, gw_out, gk = pl.pallas_call(
         flush_kernel,
         out_shape=shapes,

time: 41.7 us -> 43.1 us (1.034)
  Pallas kernels: 40.1 us -> 42.3 us
  local copies, waits for them, and re-layouts: 0.69 us -> 0 us
    pallas_call x1, Pallas kernels: 39.1 us -> 41.3 us  [fused_shards(): pl.pallas_call(functools.partial(fused_kernel, L, J, 1.0 / math.sqrt(rows...]
    unnamed x2 -> x0, local copies, waits for them, and re-layouts: 0.69 us -> none
where the time goes in v3:
time: 43.1 us; the launch traced here: 43 us
  Pallas kernels  42.3 us (98%)
  between operations  0.64 us (1%)
    pallas_call x1, Pallas kernels, fused_shards(): pl.pallas_call(functools.partial(fused_kernel, L, J, 1.0 / math.sqrt(rows...  41.3 us
    pallas_call x1, Pallas kernels, fused_shards(): pl.pallas_call(flush_kernel, out_shape=shapes, in_specs=[pl.BlockSpec(mem...  1.02 us

profile of v3, /device:TPU:0, one launch (start us, length us, event | category | flops | bytes accessed | tf_op | source)
XLA Modules:
  0.0 43.0 jit_solution(4038453925272510004)
XLA Ops:
  0.6 41.3 %shard_map.92 = (bf16[64,4096]{1,0:T(8,128)(2,1)S(1)}, bf16[64,4096]{1,0:T(8,128)(2,1)S(1)}, f32[64,128]{1,0:T(8,128)S(1)}, f32[64,128]{1,0:T(8,128)S(1)}, f32[9,64]{1,0:T(8,128)S(1)}) custom-call(bf16[64,4096]{1,0:T(8,128)(2,1)} %bitcast.5, bf16[64,4096]{1,0:T(8,128)(2,1)} %bitcast.6, f32[9,64]{1,0:T(8,128)} %taps_hbm.1, bf16[256,1024]{1,0:T(8,128)(2,1)} %win_hbm.1, ...), custom_call_target="tpu_custom_call" | custom-call | flops 3221225472 | bytes 4194304 | tf_op jit(solution)/shard_map/pallas_call | solution.py:603
  42.0 1.0 %shard_map.93 = (bf16[64,4096]{1,0:T(8,128)(2,1)}, bf16[64,4096]{1,0:T(8,128)(2,1)}, f32[64,128]{1,0:T(8,128)}, f32[64,128]{1,0:T(8,128)}, f32[9,64]{1,0:T(8,128)}) custom-call(bf16[64,4096]{1,0:T(8,128)(2,1)S(1)} %get-tuple-element.15.refs_0_, bf16[64,4096]{1,0:T(8,128)(2,1)S(1)} %get-tuple-element.16.refs_1_, f32[64,128]{1,0:T(8,128)S(1)} %get-tuple-element.17.refs_2_, ...), custom_call_target="tpu_custom_call" | custom-call | tf_op jit(solution)/shard_map/pallas_call | solution.py:614

commit v4 on v3

--- a/solution.py
+++ b/solution.py
@@ -162,7 +162,7 @@
     x_hbm, ct_hbm, taps_hbm, win_hbm, wout_hbm,
     bo_out, gx_out, gw_in_out, gw_out_out, gk_out,
     xp, ctv, tapv, win, wout, wint, woutt, tf, fb, fr, ctf, nb, nrm, istd, act, gp,
-    geb, brb, gep, brv, gfull, gsend, grecv, hf, hs, hr, sf, sb, tr, zs, tz, vf, vs, vr, gka, kt, acc_x,
+    geb, brb, gep, brv, gfull, gsend, grecv, s1s, s1r, s2s, s2r, uf, sb, tr, gka, kt, acc_x,
     load, send, recv,
 ):
     cl, rows = ctv.shape
@@ -224,7 +224,7 @@
     ge_base, br_base = take(S * (J - 1)), take(S * (J - 1))
     xh_base, gh_base = take(S * 2), take(S * 2)
     core_base = take(Z)
-    h_base, tz_base = take(Z * (J - 1)), take(Z - 1)
+    s1_base, s2_base, z_base = take(2 * Z), take(2 * Z), take(Z - 1)
 
     def ct_copies(s):
         return [rcopy(ctv.at[:, col(s, j)], ctf.at[s, mine, :], ct_base + s * (J - 1) + d, me_l, j)
@@ -385,29 +385,31 @@
 
     lax.fori_loop(0, Z, term_body, 0)
 
-    def h_copies(zz):
-        return [rcopy(hs.at[j, zz], hr.at[me_j, zz], h_base + zz * (J - 1) + d, me_l, j)
-                for d, j in enumerate(chan_peers)]
-
-    def zfirst(e):
+    jx = me_j + 1 - 2 * lax.rem(me_j, 2)
+    jy = lax.rem(me_j + 2, J)
+    jd = lax.rem(jx + 2, J)
+
+    def piece(j):
+        return pl.ds(pl.multiple_of(j * CR, CR), CR)
+
+    def s1_copies(zz):
+        return [rcopy(s1s.at[zz, i], s1r.at[zz, i], s1_base + 2 * zz + i, me_l, j) for i, j in enumerate((jx, jy))]
+
+    def s2_copies(zz):
+        return [rcopy(s2s.at[zz, i], s2r.at[zz, i], s2_base + 2 * zz + i, me_l, j) for i, j in enumerate((jy, jx))]
+
+    def z_copy(e):
         zz = lax.rem(z + 1 + e, Z)
-        return rcopy(zs.at[zz], tz.at[z], tz_base + e, zz * 2 + core, me_j)
+        return rcopy(sb.at[zz], tr.at[z], z_base + e, zz * 2 + core, me_j)
 
     def core_sum(e, carry):
         zz = lax.rem(z + 1 + e, Z)
         core_copy(zz).wait_recv()
-        h = gfull[core, zz, 1] + grecv[zz, 1].astype(f32)
-        gfull[core, zz, 1] = h
-        zs[zz] = h.astype(bf)
-
-        @pl.when(e < Z - 1)
-        def _():
-            zfirst(e).start()
-        h = gfull[core, zz, 0] + grecv[zz, 0].astype(f32)
-        for j in range(J):
-            hf[j, zz] = h[j * CR:(j + 1) * CR]
-            hs[j, zz] = h[j * CR:(j + 1) * CR].astype(bf)
-        start(h_copies(zz))
+        for i, j in enumerate((jx, jy)):
+            gfull[core, zz, i] = gfull[core, zz, i] + grecv[zz, i].astype(f32)
+            s1s[zz, i, 0] = gfull[core, zz, i, piece(j), :].astype(bf)
+            s1s[zz, i, 1] = gfull[core, zz, i, piece(jd), :].astype(bf)
+        start(s1_copies(zz))
 
         @pl.when(e == 1)
         def _():
@@ -415,8 +417,32 @@
         return carry
 
     lax.fori_loop(0, Z, core_sum, 0)
-    for s in range(1, S):
-        start(br_copies(s))
+    start(br_copies(1))
+
+    def halving(e, carry):
+        zz = lax.rem(z + 1 + e, Z)
+        arrive(s1_copies(zz))
+        for i, j in enumerate((jy, jx)):
+            s2s[zz, i] = (gfull[core, zz, i, piece(j), :] + s1r[zz, i, 1].astype(f32)).astype(bf)
+            uf[zz, i] = gfull[core, zz, i, piece(me_j), :] + s1r[zz, i, 0].astype(f32)
+        start(s2_copies(zz))
+
+        @pl.when(e == Z - 2)
+        def _():
+            start(br_copies(2))
+        return carry
+
+    def z_stage(e, carry):
+        zz = lax.rem(z + 1 + e, Z)
+        arrive(s2_copies(zz))
+        total = uf[zz] + s2r[zz].astype(f32)
+        uf[zz] = total
+        sb[zz] = total.astype(bf)
+
+        @pl.when(e < Z - 1)
+        def _():
+            z_copy(e).start()
+        return carry
 
     def early_terms(s, carry):
         kernel_terms(s)
@@ -457,32 +483,11 @@
     for s in range(S - 1):
         arrive(gh_copies(s))
     back(False)
+    lax.fori_loop(0, Z, halving, 0)
+    start(br_copies(3))
     arrive(gh_copies(S - 1))
     back(True)
-
-    for zz in range(Z):
-        arrive(h_copies(zz))
-    for zz in range(Z):
-        total = hf[me_j, zz]
-        for d in range(1, J):
-            total = total + hr[lax.rem(me_j + J - d, J), zz].astype(f32)
-        sf[zz] = total
-        sb[zz] = total.astype(bf)
-    z_in = []
-    for e in range(1, Z):
-        zz = lax.rem(z + e, Z)
-        z_in.append(rcopy(sb.at[zz], tr.at[z], take(), zz * 2 + core, me_j))
-    start(z_in)
-    for e in range(Z - 1):
-        zfirst(e).wait_recv()
-    total = gfull[core, z, 1]
-    for e in range(1, Z):
-        total = total + tz[lax.rem(z + Z - e, Z)].astype(f32)
-    for j in range(J):
-        vf[j] = total[j * CR:(j + 1) * CR]
-        vs[j] = total[j * CR:(j + 1) * CR].astype(bf)
-    v_in = [rcopy(vs.at[j], vr.at[me_j], take(), me_l, j) for j in chan_peers]
-    start(v_in)
+    lax.fori_loop(0, Z, z_stage, 0)
 
     def finish(s, carry):
         arrive(br_copies(s))
@@ -496,16 +501,13 @@
     for l in range(1, L):
         total = total + kt[l]
     gk_out[...] = total[0:TAPS, 0:cl]
-    arrive(z_in)
-    total = sf[z]
+    for e in range(Z - 1):
+        z_copy(e).wait_recv()
+    total = uf[z]
     for e in range(1, Z):
         total = total + tr[lax.rem(z + Z - e, Z)].astype(f32)
-    gw_in_out[...] = total
-    arrive(v_in)
-    total = vf[me_j]
-    for d in range(1, J):
-        total = total + vr[lax.rem(me_j + J - d, J)].astype(f32)
-    gw_out_out[...] = total
+    gw_in_out[...] = total[0]
+    gw_out_out[...] = total[1]
 
     def sent(s, carry):
         for copies in (ct_copies(s), f_copies(s), ge_copies(s), br_copies(s), xh_copies(s), gh_copies(s)):
@@ -515,9 +517,9 @@
 
     lax.fori_loop(0, S, sent, 0)
     for zz in range(Z):
-        for c in [core_copy(zz)] + h_copies(zz):
+        for c in [core_copy(zz)] + s1_copies(zz) + s2_copies(zz):
             c.wait_send()
-    for c in kt_in + z_in + v_in + [zfirst(e) for e in range(Z - 1)]:
+    for c in kt_in + [z_copy(e) for e in range(Z - 1)]:
         c.wait_send()
 
 
@@ -574,22 +576,18 @@
         pltpu.VMEM((2, Z, 2, C, 128), f32),
         pltpu.VMEM((2, Z, 2, C, 128), bf),
         pltpu.VMEM((Z, 2, C, 128), bf),
-        pltpu.VMEM((J, Z, CR, 128), f32),
-        pltpu.VMEM((J, Z, CR, 128), bf),
-        pltpu.VMEM((J, Z, CR, 128), bf),
-        pltpu.VMEM((Z, CR, 128), f32),
-        pltpu.VMEM((Z, CR, 128), bf),
-        pltpu.VMEM((Z, CR, 128), bf),
-        pltpu.VMEM((Z, C, 128), bf),
-        pltpu.VMEM((Z, C, 128), bf),
-        pltpu.VMEM((J, CR, 128), f32),
-        pltpu.VMEM((J, CR, 128), bf),
-        pltpu.VMEM((J, CR, 128), bf),
+        pltpu.VMEM((Z, 2, 2, CR, 128), bf),
+        pltpu.VMEM((Z, 2, 2, CR, 128), bf),
+        pltpu.VMEM((Z, 2, CR, 128), bf),
+        pltpu.VMEM((Z, 2, CR, 128), bf),
+        pltpu.VMEM((Z, 2, CR, 128), f32),
+        pltpu.VMEM((Z, 2, CR, 128), bf),
+        pltpu.VMEM((Z, 2, CR, 128), bf),
         pltpu.VMEM((TAPS, cl, 128), f32),
         pltpu.VMEM((L, 16, 128), f32),
         pltpu.VMEM((cl, rows), f32),
     ]
-    copies = 4 * S * (J - 1) + 4 * S + Z + (Z + 1) * (J - 1) + (L - 1) + 2 * (Z - 1)
+    copies = 4 * S * (J - 1) + 4 * S + 5 * Z + (L - 1) + (Z - 1)
     scratch += [pltpu.SemaphoreType.DMA((5,)), pltpu.SemaphoreType.DMA((copies,)), pltpu.SemaphoreType.DMA((copies,))]
     vmem = pl.BlockSpec(memory_space=pltpu.VMEM)
     hbm = pl.BlockSpec(memory_space=HBM)

time: 43.1 us -> 40.4 us (0.937)
  Pallas kernels: 42.3 us -> 39.6 us
    pallas_call x1, Pallas kernels: 41.3 us -> 38.6 us  [fused_shards(): pl.pallas_call(functools.partial(fused_kernel, L, J, 1.0 / math.sqrt(rows...]
where the time goes in v4:
time: 40.4 us; the launch traced here: 40.2 us
  Pallas kernels  39.6 us (98%)
  between operations  0.64 us (2%)
    pallas_call x1, Pallas kernels, fused_shards(): pl.pallas_call(functools.partial(fused_kernel, L, J, 1.0 / math.sqrt(rows...  38.6 us
    pallas_call x1, Pallas kernels, fused_shards(): pl.pallas_call(flush_kernel, out_shape=shapes, in_specs=[pl.BlockSpec(mem...  1.02 us

profile of v4, /device:TPU:0, one launch (start us, length us, event | category | flops | bytes accessed | tf_op | source)
XLA Modules:
  0.0 40.2 jit_solution(17599972030779732897)
XLA Ops:
  0.6 38.6 %shard_map.92 = (bf16[64,4096]{1,0:T(8,128)(2,1)S(1)}, bf16[64,4096]{1,0:T(8,128)(2,1)S(1)}, f32[64,128]{1,0:T(8,128)S(1)}, f32[64,128]{1,0:T(8,128)S(1)}, f32[9,64]{1,0:T(8,128)S(1)}) custom-call(bf16[64,4096]{1,0:T(8,128)(2,1)} %bitcast.5, bf16[64,4096]{1,0:T(8,128)(2,1)} %bitcast.6, f32[9,64]{1,0:T(8,128)} %taps_hbm.1, bf16[256,1024]{1,0:T(8,128)(2,1)} %win_hbm.1, ...), custom_call_target="tpu_custom_call" | custom-call | flops 3221225472 | bytes 4194304 | tf_op jit(solution)/shard_map/pallas_call | solution.py:601
  39.2 1.0 %shard_map.93 = (bf16[64,4096]{1,0:T(8,128)(2,1)}, bf16[64,4096]{1,0:T(8,128)(2,1)}, f32[64,128]{1,0:T(8,128)}, f32[64,128]{1,0:T(8,128)}, f32[9,64]{1,0:T(8,128)}) custom-call(bf16[64,4096]{1,0:T(8,128)(2,1)S(1)} %get-tuple-element.15.refs_0_, bf16[64,4096]{1,0:T(8,128)(2,1)S(1)} %get-tuple-element.16.refs_1_, f32[64,128]{1,0:T(8,128)S(1)} %get-tuple-element.17.refs_2_, ...), custom_call_target="tpu_custom_call" | custom-call | tf_op jit(solution)/shard_map/pallas_call | solution.py:612

commit v5 on v4

--- a/solution.py
+++ b/solution.py
@@ -162,7 +162,7 @@
     x_hbm, ct_hbm, taps_hbm, win_hbm, wout_hbm,
     bo_out, gx_out, gw_in_out, gw_out_out, gk_out,
     xp, ctv, tapv, win, wout, wint, woutt, tf, fb, fr, ctf, nb, nrm, istd, act, gp,
-    geb, brb, gep, brv, gfull, gsend, grecv, s1s, s1r, s2s, s2r, uf, sb, tr, gka, kt, acc_x,
+    geb, brb, gep, brv, gfull, gsend, grecv, s1s, s1r, s2s, s2r, uf, sb, tr, gka, kt, kr, acc_x,
     load, send, recv,
 ):
     cl, rows = ctv.shape
@@ -171,31 +171,35 @@
     K = rows // B
     S = K // 2
     W = 2 * B // J
+    V = (J - 1) * cl
     Z = L // 2
     own = MIDDLE * B
     bf, f32 = jnp.bfloat16, jnp.float32
     me_l, me_j = lax.axis_index("loop"), lax.axis_index("chan")
     core, z = lax.rem(me_l, 2), me_l // 2
-    used = [0]
-
-    def take(n=1):
-        used[0] += n
-        return used[0] - n
-
-    def rcopy(src, dst, idx, l, j):
+    ct_r, f_r, ge_r, xh_r, core_r, s1_r, s2_r = [S * i for i in range(7)]
+    br_r = 7 * S
+    gh_r, z_r, kt_r = br_r + 2, br_r + 4, br_r + 5
+    ct_s, f_s, ge_s, br_s, xh_s, gh_s, core_s, s1_s, s2_s, z_s, kt_s = range(11)
+
+    def rcopy(src, dst, out, into, l, j):
         return pltpu.make_async_remote_copy(
-            src_ref=src, dst_ref=dst, send_sem=send.at[idx], recv_sem=recv.at[idx],
+            src_ref=src, dst_ref=dst, send_sem=send.at[out], recv_sem=recv.at[into],
             device_id=(l, j), device_id_type=MESH)
+
+    def await_all(like, sem):
+        pltpu.make_async_copy(like, like, sem).wait()
+
+    def got(like, into):
+        await_all(like, recv.at[into])
 
     def lanes(at, n):
         return pl.ds(pl.multiple_of(at, 128), n)
 
-    loads = [pltpu.make_async_copy(a, b, load.at[i]) for i, (a, b) in enumerate((
-        (x_hbm, xp.at[:, own:own + rows]), (ct_hbm, ctv), (taps_hbm, tapv), (win_hbm, win), (wout_hbm, wout)))]
-    for c in loads:
-        c.start()
-
-    chan_peers = [lax.rem(me_j + d, J) for d in range(1, J)]
+    jx = me_j + 1 - 2 * lax.rem(me_j, 2)
+    jy = lax.rem(me_j + 2, J)
+    jd = lax.rem(jx + 2, J)
+    chan_peers = [jd, jx, jy]
     loop_peers = [lax.rem(me_l + e, L) for e in range(1, L)]
     right, left = loop_peers[0], loop_peers[-1]
 
@@ -205,6 +209,11 @@
     for l in loop_peers:
         pl.semaphore_signal(barrier, inc=1, device_id=(l, me_j), device_id_type=MESH)
 
+    loads = [pltpu.make_async_copy(a, b, load.at[i]) for i, (a, b) in enumerate((
+        (x_hbm, xp.at[:, own:own + rows]), (ct_hbm, ctv), (taps_hbm, tapv), (win_hbm, win), (wout_hbm, wout)))]
+    for c in loads[:3]:
+        c.start()
+
     half = J // 2
     mine = pl.ds(pl.multiple_of(me_j * cl, cl), cl)
 
@@ -220,55 +229,42 @@
     def chan_rows(j):
         return pl.ds(pl.multiple_of(j * cl, cl), cl)
 
-    ct_base, f_base = take(S * (J - 1)), take(S * (J - 1))
-    ge_base, br_base = take(S * (J - 1)), take(S * (J - 1))
-    xh_base, gh_base = take(S * 2), take(S * 2)
-    core_base = take(Z)
-    s1_base, s2_base, z_base = take(2 * Z), take(2 * Z), take(Z - 1)
-
     def ct_copies(s):
-        return [rcopy(ctv.at[:, col(s, j)], ctf.at[s, mine, :], ct_base + s * (J - 1) + d, me_l, j)
-                for d, j in enumerate(chan_peers)]
+        return [rcopy(ct_hbm.at[:, col(s, j)], ctf.at[s, mine, :], ct_s, ct_r + s, me_l, j) for j in chan_peers]
 
     def f_copies(s):
-        return [rcopy(fb.at[:, col(s, j)], fr.at[s, mine, :], f_base + s * (J - 1) + d, me_l, j)
-                for d, j in enumerate(chan_peers)]
+        return [rcopy(fb.at[:, col(s, j)], fr.at[s, mine, :], f_s, f_r + s, me_l, j) for j in chan_peers]
 
     def ge_copies(s):
-        return [rcopy(geb.at[s, chan_rows(j), :], gep.at[:, own_col(s, me_j)], ge_base + s * (J - 1) + d, me_l, j)
-                for d, j in enumerate(chan_peers)]
+        return [rcopy(geb.at[s, chan_rows(j), :], gep.at[:, own_col(s, me_j)], ge_s, ge_r + s, me_l, j)
+                for j in chan_peers]
 
     def br_copies(s):
-        return [rcopy(brb.at[s, chan_rows(j), :], brv.at[:, col(s, me_j)], br_base + s * (J - 1) + d, me_l, j)
-                for d, j in enumerate(chan_peers)]
-
-    def halo_copies(buf, right_block, left_block, base):
-        return [rcopy(buf.at[:, block(right_block + S)], buf.at[:, block(right_block - S)], base, right, me_j),
-                rcopy(buf.at[:, block(left_block + S)], buf.at[:, block(left_block + K + S)], base + 1, left, me_j)]
+        return [rcopy(brb.at[s, chan_rows(j), :], brv.at[:, col(s, me_j)], br_s, br_r + s // (S - 1), me_l, j)
+                for j in chan_peers]
 
     def xh_copies(s):
-        return halo_copies(xp, K - 1 - s, s, xh_base + 2 * s)
+        return [rcopy(x_hbm.at[:, block(K - 1 - s)], xp.at[:, block(S - 1 - s)], xh_s, xh_r + s, right, me_j),
+                rcopy(x_hbm.at[:, block(s)], xp.at[:, block(K + S + s)], xh_s, xh_r + s, left, me_j)]
 
     def gh_copies(s):
-        return halo_copies(gep, S + s, S - 1 - s, gh_base + 2 * s)
+        near, far, into = S - 1 - s, S + s, gh_r + s // (S - 1)
+        return [rcopy(gep.at[:, block(far + S)], gep.at[:, block(far - S)], gh_s, into, right, me_j),
+                rcopy(gep.at[:, block(near + S)], gep.at[:, block(near + K + S)], gh_s, into, left, me_j)]
 
     def start(copies):
         for c in copies:
             c.start()
 
-    def arrive(copies):
-        for c in copies:
-            c.wait_recv()
-
-    loads[0].wait()
-    loads[1].wait()
     pl.semaphore_wait(barrier, J - 1 + L - 1)
-    for s in range(S):
+    start(xh_copies(0))
+    start(ct_copies(0))
+    for s in range(1, S):
         start(xh_copies(s))
-    for s in range(S - 1):
         start(ct_copies(s))
-
-    for c in loads[2:]:
+    for c in loads[3:]:
+        c.start()
+    for c in loads:
         c.wait()
     padded = jnp.concatenate([tapv[...], jnp.zeros((128 - TAPS, cl), f32)], axis=0)
     columns = jnp.concatenate([padded, jnp.zeros((128, 128 - cl), f32)], axis=1).T
@@ -280,30 +276,37 @@
     for s in range(S):
         ctf[s, mine, :] = ctv[:, col(s, me_j)]
 
-    def conv_body(s, carry):
-        arrive(xh_copies(s))
-        for g in range(cl // 16):
-            ch = slice(g * 16, (g + 1) * 16)
-            w = [tf[t, ch, :] for t in range(TAPS)]
-            for k in (S - 1 - s, S + s):
-                for q in range(B // 128):
-                    acc = jnp.zeros((16, 128), f32)
-                    for t in range(TAPS):
-                        acc = acc + w[t] * xp[ch, lanes((k + t) * B + q * 128, 128)].astype(f32)
-                    fb[ch, lanes(k * B + q * 128, 128)] = acc.astype(bf)
+    def conv(s):
+        near, far = S - 1 - s, S + s
+
+        def part(q, carry):
+            done = []
+            for g in range(cl // 16):
+                ch = slice(g * 16, (g + 1) * 16)
+                w = [tf[t, ch, :] for t in range(TAPS)]
+                sums = [jnp.zeros((16, 128), f32) for _ in range(2)]
+                for b in range(near, far + TAPS):
+                    v = xp[ch, lanes(b * B + q * 128, 128)].astype(f32)
+                    for i, k in enumerate((near, far)):
+                        if 0 <= b - k < TAPS:
+                            sums[i] = sums[i] + w[b - k] * v
+                done.append([a.astype(bf) for a in sums])
+            for g in range(cl // 16):
+                for i, k in enumerate((near, far)):
+                    fb[g * 16:(g + 1) * 16, lanes(k * B + q * 128, 128)] = done[g][i]
+            return carry
+
+        lax.fori_loop(0, B // 128, part, 0)
+
+    for s in range(S):
+        got(xp.at[:, 0:2 * B], xh_r + s)
+        conv(s)
         start(f_copies(s))
         fr[s, mine, :] = fb[:, col(s, me_j)]
 
-        @pl.when(s == 0)
-        def _():
-            start(ct_copies(S - 1))
-        return carry
-
-    lax.fori_loop(0, S, conv_body, 0)
-
     def mlp_body(s, carry):
-        arrive(ct_copies(s))
-        arrive(f_copies(s))
+        got(ctf.at[s, 0:V, :], ct_r + s)
+        got(fr.at[s, 0:V, :], f_r + s)
         here = lanes(s * W, W)
         for b in range(W // 128):
             part = slice(b * 128, (b + 1) * 128)
@@ -342,29 +345,30 @@
         return carry
 
     lax.fori_loop(0, S, mlp_body, 0)
-    start(br_copies(0))
 
     def forward(s):
-        arrive(ge_copies(s))
+        got(gep.at[:, 0:(J - 1) * W], ge_r + s)
         start(gh_copies(s))
 
     def kernel_terms(s):
+        near, far = S - 1 - s, S + s
         for g in range(cl // 16):
             ch = slice(g * 16, (g + 1) * 16)
             sums = [gka[t, ch, :] for t in range(TAPS)]
-            for k in (S - 1 - s, S + s):
-                for q in range(B // 128):
-                    e = gep[ch, lanes(own + k * B + q * 128, 128)].astype(f32)
-                    for t in range(TAPS):
-                        sums[t] = sums[t] + e * xp[ch, lanes((k + t) * B + q * 128, 128)].astype(f32)
+            for q in range(B // 128):
+                e = [gep[ch, lanes(own + k * B + q * 128, 128)].astype(f32) for k in (near, far)]
+                for b in range(near, far + TAPS):
+                    v = xp[ch, lanes(b * B + q * 128, 128)].astype(f32)
+                    for i, k in enumerate((near, far)):
+                        if 0 <= b - k < TAPS:
+                            sums[b - k] = sums[b - k] + e[i] * v
             for t in range(TAPS):
                 gka[t, ch, :] = sums[t]
 
-    forward(0)
     CR = C // J
 
     def core_copy(zz):
-        return rcopy(gsend.at[1 - core, zz], grecv.at[zz], core_base + zz, z * 2 + 1 - core, me_j)
+        return rcopy(gsend.at[1 - core, zz], grecv.at[zz], core_s, core_r + zz, z * 2 + 1 - core, me_j)
 
     def term_body(e, carry):
         zz = lax.rem(z + 1 + e, Z)
@@ -378,149 +382,137 @@
                 gsend[h, zz, i] = part.astype(bf)
         core_copy(zz).start()
 
-        @pl.when(e == 1)
+        @pl.when(e == 2)
         def _():
             forward(1)
+
+        @pl.when(e >= 2)
+        def _():
+            core_sum(e - 2)
         return carry
-
-    lax.fori_loop(0, Z, term_body, 0)
-
-    jx = me_j + 1 - 2 * lax.rem(me_j, 2)
-    jy = lax.rem(me_j + 2, J)
-    jd = lax.rem(jx + 2, J)
 
     def piece(j):
         return pl.ds(pl.multiple_of(j * CR, CR), CR)
 
     def s1_copies(zz):
-        return [rcopy(s1s.at[zz, i], s1r.at[zz, i], s1_base + 2 * zz + i, me_l, j) for i, j in enumerate((jx, jy))]
+        return [rcopy(s1s.at[zz, i], s1r.at[zz, i], s1_s, s1_r + zz, me_l, j) for i, j in enumerate((jx, jy))]
 
     def s2_copies(zz):
-        return [rcopy(s2s.at[zz, i], s2r.at[zz, i], s2_base + 2 * zz + i, me_l, j) for i, j in enumerate((jy, jx))]
+        return [rcopy(s2s.at[zz, i], s2r.at[zz, i], s2_s, s2_r + zz, me_l, j) for i, j in enumerate((jy, jx))]
 
     def z_copy(e):
         zz = lax.rem(z + 1 + e, Z)
-        return rcopy(sb.at[zz], tr.at[z], z_base + e, zz * 2 + core, me_j)
-
-    def core_sum(e, carry):
+        return rcopy(sb.at[zz], tr.at[z - (z > zz).astype(jnp.int32)], z_s, z_r, zz * 2 + core, me_j)
+
+    def core_sum(e):
         zz = lax.rem(z + 1 + e, Z)
-        core_copy(zz).wait_recv()
+        got(grecv.at[zz], core_r + zz)
         for i, j in enumerate((jx, jy)):
             gfull[core, zz, i] = gfull[core, zz, i] + grecv[zz, i].astype(f32)
             s1s[zz, i, 0] = gfull[core, zz, i, piece(j), :].astype(bf)
             s1s[zz, i, 1] = gfull[core, zz, i, piece(jd), :].astype(bf)
         start(s1_copies(zz))
 
-        @pl.when(e == 1)
-        def _():
-            forward(2)
-        return carry
-
-    lax.fori_loop(0, Z, core_sum, 0)
-    start(br_copies(1))
-
-    def halving(e, carry):
+    def halving(e):
         zz = lax.rem(z + 1 + e, Z)
-        arrive(s1_copies(zz))
+        got(s1r.at[zz], s1_r + zz)
         for i, j in enumerate((jy, jx)):
             s2s[zz, i] = (gfull[core, zz, i, piece(j), :] + s1r[zz, i, 1].astype(f32)).astype(bf)
             uf[zz, i] = gfull[core, zz, i, piece(me_j), :] + s1r[zz, i, 0].astype(f32)
         start(s2_copies(zz))
 
-        @pl.when(e == Z - 2)
-        def _():
-            start(br_copies(2))
-        return carry
-
-    def z_stage(e, carry):
+    def z_stage(e):
         zz = lax.rem(z + 1 + e, Z)
-        arrive(s2_copies(zz))
+        got(s2r.at[zz], s2_r + zz)
         total = uf[zz] + s2r[zz].astype(f32)
         uf[zz] = total
         sb[zz] = total.astype(bf)
 
-        @pl.when(e < Z - 1)
-        def _():
+        if e < Z - 1:
             z_copy(e).start()
-        return carry
-
-    def early_terms(s, carry):
-        kernel_terms(s)
-        return carry
-
-    lax.fori_loop(0, S - 1, early_terms, 0)
-    forward(S - 1)
-    kernel_terms(S - 1)
+
+    def back(final):
+        late = (S - 1, S, S + K - 1, S + K)
+
+        def part(q, carry):
+            for g in range(cl // 16):
+                ch = slice(g * 16, (g + 1) * 16)
+                w = [tf[t, ch, :] for t in range(TAPS)]
+                at = [lanes(k * B + q * 128, 128) for k in range(K)]
+                sums = [acc_x[ch, a] if final else ctv[ch, a].astype(f32) for a in at]
+                for b in range(K + 2 * S):
+                    if (b in late) == final:
+                        v = gep[ch, lanes(b * B + q * 128, 128)].astype(f32)
+                        for t in range(TAPS):
+                            k = b - (TAPS - 1 - t)
+                            if 0 <= k < K:
+                                sums[k] = sums[k] + w[t] * v
+                for k in range(K):
+                    if final:
+                        gx_out[ch, at[k]] = sums[k].astype(bf)
+                    else:
+                        acc_x[ch, at[k]] = sums[k]
+            return carry
+
+        lax.fori_loop(0, B // 128, part, 0)
+
+    forward(0)
+    lax.fori_loop(0, Z, term_body, 0)
+    core_sum(Z - 2)
+    kernel_terms(0)
+    core_sum(Z - 1)
+    start(br_copies(0))
+    start(br_copies(1))
+    kernel_terms(1)
+    forward(2)
+    kernel_terms(2)
+    forward(3)
+    halving(0)
+    kernel_terms(3)
+    halving(1)
     sums = [jnp.sum(gka[t], axis=1, keepdims=True) * grad_scale for t in range(TAPS)]
     total = jnp.concatenate(sums + [jnp.zeros((cl, 128 - TAPS), f32)], axis=1)
     total = jnp.concatenate([total, jnp.zeros((128 - cl, 128), f32)], axis=0).T
     kt[me_l] = total[0:16]
-    kt_in = [rcopy(kt.at[me_l], kt.at[me_l], take(), l, me_j) for l in loop_peers]
-    start(kt_in)
-
-    def back(final):
-        late = (S - 1, S, S + K - 1, S + K)
-
-        def part(q, carry):
-            for g in range(cl // 16):
-                ch = slice(g * 16, (g + 1) * 16)
-                w = [tf[t, ch, :] for t in range(TAPS)]
-                for k in range(K):
-                    at = lanes(k * B + q * 128, 128)
-                    acc = acc_x[ch, at] if final else ctv[ch, at].astype(f32)
-                    for t in range(TAPS):
-                        b = k + TAPS - 1 - t
-                        if (b in late) == final:
-                            acc = acc + w[t] * gep[ch, lanes(b * B + q * 128, 128)].astype(f32)
-                    if final:
-                        gx_out[ch, at] = acc.astype(bf)
-                    else:
-                        acc_x[ch, at] = acc
-            return carry
-
-        lax.fori_loop(0, B // 128, part, 0)
-
-    for s in range(S - 1):
-        arrive(gh_copies(s))
+    start([rcopy(kt.at[me_l], kr.at[me_l - (me_l > l).astype(jnp.int32)], kt_s, kt_r, l, me_j) for l in loop_peers])
+
+    halving(2)
+    start(br_copies(2))
+    halving(3)
+    start(br_copies(3))
+    z_stage(0)
+    got(gep.at[:, 0:(S - 1) * 2 * B], gh_r)
     back(False)
-    lax.fori_loop(0, Z, halving, 0)
-    start(br_copies(3))
-    arrive(gh_copies(S - 1))
+    z_stage(1)
+    z_stage(2)
+    got(gep.at[:, 0:2 * B], gh_r + 1)
     back(True)
-    lax.fori_loop(0, Z, z_stage, 0)
-
-    def finish(s, carry):
-        arrive(br_copies(s))
-        for k in (S - 1 - s, S + s):
-            bo_out[:, block(k)] = (xp[:, block(k + S)].astype(f32) + brv[:, block(k)].astype(f32)).astype(bf)
+    z_stage(3)
+
+    def finish(k, carry):
+        bo_out[:, block(k)] = (xp[:, block(k + S)].astype(f32) + brv[:, block(k)].astype(f32)).astype(bf)
         return carry
 
-    lax.fori_loop(0, S, finish, 0)
-    arrive(kt_in)
-    total = kt[0]
-    for l in range(1, L):
-        total = total + kt[l]
+    got(brv.at[:, 0:(S - 1) * (J - 1) * W], br_r)
+    lax.fori_loop(1, K - 1, finish, 0)
+    got(kr, kt_r)
+    total = kt[me_l]
+    for l in range(L - 1):
+        total = total + kr[l]
     gk_out[...] = total[0:TAPS, 0:cl]
+    got(brv.at[:, 0:(J - 1) * W], br_r + 1)
+    finish(0, 0)
+    finish(K - 1, 0)
+    got(tr, z_r)
+    total = uf[z]
     for e in range(Z - 1):
-        z_copy(e).wait_recv()
-    total = uf[z]
-    for e in range(1, Z):
-        total = total + tr[lax.rem(z + Z - e, Z)].astype(f32)
+        total = total + tr[e].astype(f32)
     gw_in_out[...] = total[0]
     gw_out_out[...] = total[1]
-
-    def sent(s, carry):
-        for copies in (ct_copies(s), f_copies(s), ge_copies(s), br_copies(s), xh_copies(s), gh_copies(s)):
-            for c in copies:
-                c.wait_send()
-        return carry
-
-    lax.fori_loop(0, S, sent, 0)
-    for zz in range(Z):
-        for c in [core_copy(zz)] + s1_copies(zz) + s2_copies(zz):
-            c.wait_send()
-    for c in kt_in + [z_copy(e) for e in range(Z - 1)]:
-        c.wait_send()
+    for like, out in ((ctv.at[:, 0:S * (J - 1) * W], ct_s), (fb.at[:, 0:S * (J - 1) * W], f_s), (geb.at[:, 0:V, :], ge_s),
+                      (brb.at[:, 0:V, :], br_s), (xp.at[:, 0:2 * S * B], xh_s), (gep.at[:, 0:2 * S * B], gh_s),
+                      (gsend.at[0], core_s), (s1s, s1_s), (s2s, s2_s), (sb.at[0:Z - 1], z_s), (kt.at[0:L - 1], kt_s)):
+        await_all(like, send.at[out])
 
 
 def flush_kernel(*refs):
@@ -535,7 +527,7 @@
 
 def fits(L, J, rows, cl, F):
     return (cl * 2 == 128 and rows == 2 * MIDDLE * DILATION_STEP and L % 2 == 0 and L > 2 and J == 4
-            and F == L * 128)
+            and F == L * 128 and L == 2 * MIDDLE)
 
 
 def fused_shards(features, kernel_tap_rows, in_weight, out_weight, cotangent):
@@ -582,13 +574,13 @@
         pltpu.VMEM((Z, 2, CR, 128), bf),
         pltpu.VMEM((Z, 2, CR, 128), f32),
         pltpu.VMEM((Z, 2, CR, 128), bf),
-        pltpu.VMEM((Z, 2, CR, 128), bf),
+        pltpu.VMEM((Z - 1, 2, CR, 128), bf),
         pltpu.VMEM((TAPS, cl, 128), f32),
         pltpu.VMEM((L, 16, 128), f32),
+        pltpu.VMEM((L - 1, 16, 128), f32),
         pltpu.VMEM((cl, rows), f32),
     ]
-    copies = 4 * S * (J - 1) + 4 * S + 5 * Z + (L - 1) + (Z - 1)
-    scratch += [pltpu.SemaphoreType.DMA((5,)), pltpu.SemaphoreType.DMA((copies,)), pltpu.SemaphoreType.DMA((copies,))]
+    scratch += [pltpu.SemaphoreType.DMA((5,)), pltpu.SemaphoreType.DMA((11,)), pltpu.SemaphoreType.DMA((7 * S + 6,))]
     vmem = pl.BlockSpec(memory_space=pltpu.VMEM)
     hbm = pl.BlockSpec(memory_space=HBM)
     shapes = (

time: 40.4 us -> 39.4 us (0.975)
  Pallas kernels: 39.6 us -> 38.6 us
    pallas_call x1, Pallas kernels: 38.6 us -> 37.6 us  [fused_shards(): pl.pallas_call(functools.partial(fused_kernel, L, J, 1.0 / math.sqrt(rows...]
where the time goes in v5:
time: 39.4 us; the launch traced here: 39.2 us
  Pallas kernels  38.6 us (98%)
  between operations  0.64 us (2%)
    pallas_call x1, Pallas kernels, fused_shards(): pl.pallas_call(functools.partial(fused_kernel, L, J, 1.0 / math.sqrt(rows...  37.6 us
    pallas_call x1, Pallas kernels, fused_shards(): pl.pallas_call(flush_kernel, out_shape=shapes, in_specs=[pl.BlockSpec(mem...  1.02 us

profile of v5, /device:TPU:0, one launch (start us, length us, event | category | flops | bytes accessed | tf_op | source)
XLA Modules:
  0.0 39.2 jit_solution(10834634301645106091)
XLA Ops:
  0.6 37.6 %shard_map.92 = (bf16[64,4096]{1,0:T(8,128)(2,1)S(1)}, bf16[64,4096]{1,0:T(8,128)(2,1)S(1)}, f32[64,128]{1,0:T(8,128)S(1)}, f32[64,128]{1,0:T(8,128)S(1)}, f32[9,64]{1,0:T(8,128)S(1)}) custom-call(bf16[64,4096]{1,0:T(8,128)(2,1)} %bitcast.5, bf16[64,4096]{1,0:T(8,128)(2,1)} %bitcast.6, f32[9,64]{1,0:T(8,128)} %taps_hbm.1, bf16[256,1024]{1,0:T(8,128)(2,1)} %win_hbm.1, ...), custom_call_target="tpu_custom_call" | custom-call | flops 3221225472 | bytes 4194304 | tf_op jit(solution)/shard_map/pallas_call | solution.py:593
  38.2 1.0 %shard_map.93 = (bf16[64,4096]{1,0:T(8,128)(2,1)}, bf16[64,4096]{1,0:T(8,128)(2,1)}, f32[64,128]{1,0:T(8,128)}, f32[64,128]{1,0:T(8,128)}, f32[9,64]{1,0:T(8,128)}) custom-call(bf16[64,4096]{1,0:T(8,128)(2,1)S(1)} %get-tuple-element.15.refs_0_, bf16[64,4096]{1,0:T(8,128)(2,1)S(1)} %get-tuple-element.16.refs_1_, f32[64,128]{1,0:T(8,128)S(1)} %get-tuple-element.17.refs_2_, ...), custom_call_target="tpu_custom_call" | custom-call | tf_op jit(solution)/shard_map/pallas_call | solution.py:604

commit v6 on v5

--- a/solution.py
+++ b/solution.py
@@ -462,7 +462,6 @@
     kernel_terms(0)
     core_sum(Z - 1)
     start(br_copies(0))
-    start(br_copies(1))
     kernel_terms(1)
     forward(2)
     kernel_terms(2)
@@ -477,12 +476,13 @@
     start([rcopy(kt.at[me_l], kr.at[me_l - (me_l > l).astype(jnp.int32)], kt_s, kt_r, l, me_j) for l in loop_peers])
 
     halving(2)
+    start(br_copies(1))
     start(br_copies(2))
     halving(3)
     start(br_copies(3))
-    z_stage(0)
     got(gep.at[:, 0:(S - 1) * 2 * B], gh_r)
     back(False)
+    z_stage(0)
     z_stage(1)
     z_stage(2)
     got(gep.at[:, 0:2 * B], gh_r + 1)
@@ -500,9 +500,6 @@
     for l in range(L - 1):
         total = total + kr[l]
     gk_out[...] = total[0:TAPS, 0:cl]
-    got(brv.at[:, 0:(J - 1) * W], br_r + 1)
-    finish(0, 0)
-    finish(K - 1, 0)
     got(tr, z_r)
     total = uf[z]
     for e in range(Z - 1):
@@ -513,6 +510,9 @@
                       (brb.at[:, 0:V, :], br_s), (xp.at[:, 0:2 * S * B], xh_s), (gep.at[:, 0:2 * S * B], gh_s),
                       (gsend.at[0], core_s), (s1s, s1_s), (s2s, s2_s), (sb.at[0:Z - 1], z_s), (kt.at[0:L - 1], kt_s)):
         await_all(like, send.at[out])
+    got(brv.at[:, 0:(J - 1) * W], br_r + 1)
+    finish(0, 0)
+    finish(K - 1, 0)
 
 
 def flush_kernel(*refs):

time: 39.4 us -> 38.7 us (0.982)
  Pallas kernels: 38.6 us -> 37.9 us
    pallas_call x1, Pallas kernels: 37.6 us -> 36.9 us  [fused_shards(): pl.pallas_call(functools.partial(fused_kernel, L, J, 1.0 / math.sqrt(rows...]
where the time goes in v6:
time: 38.7 us; the launch traced here: 38.5 us
  Pallas kernels  37.9 us (98%)
  between operations  0.64 us (2%)
    pallas_call x1, Pallas kernels, fused_shards(): pl.pallas_call(functools.partial(fused_kernel, L, J, 1.0 / math.sqrt(rows...  36.9 us
    pallas_call x1, Pallas kernels, fused_shards(): pl.pallas_call(flush_kernel, out_shape=shapes, in_specs=[pl.BlockSpec(mem...  1.02 us

profile of v6, /device:TPU:0, one launch (start us, length us, event | category | flops | bytes accessed | tf_op | source)
XLA Modules:
  0.0 38.5 jit_solution(3509513645846976096)
XLA Ops:
  0.6 36.9 %shard_map.92 = (bf16[64,4096]{1,0:T(8,128)(2,1)S(1)}, bf16[64,4096]{1,0:T(8,128)(2,1)S(1)}, f32[64,128]{1,0:T(8,128)S(1)}, f32[64,128]{1,0:T(8,128)S(1)}, f32[9,64]{1,0:T(8,128)S(1)}) custom-call(bf16[64,4096]{1,0:T(8,128)(2,1)} %bitcast.5, bf16[64,4096]{1,0:T(8,128)(2,1)} %bitcast.6, f32[9,64]{1,0:T(8,128)} %taps_hbm.1, bf16[256,1024]{1,0:T(8,128)(2,1)} %win_hbm.1, ...), custom_call_target="tpu_custom_call" | custom-call | flops 3221225472 | bytes 4194304 | tf_op jit(solution)/shard_map/pallas_call | solution.py:593
  37.5 1.0 %shard_map.93 = (bf16[64,4096]{1,0:T(8,128)(2,1)}, bf16[64,4096]{1,0:T(8,128)(2,1)}, f32[64,128]{1,0:T(8,128)}, f32[64,128]{1,0:T(8,128)}, f32[9,64]{1,0:T(8,128)}) custom-call(bf16[64,4096]{1,0:T(8,128)(2,1)S(1)} %get-tuple-element.15.refs_0_, bf16[64,4096]{1,0:T(8,128)(2,1)S(1)} %get-tuple-element.16.refs_1_, f32[64,128]{1,0:T(8,128)S(1)} %get-tuple-element.17.refs_2_, ...), custom_call_target="tpu_custom_call" | custom-call | tf_op jit(solution)/shard_map/pallas_call | solution.py:604

commit v7 on v6

--- a/solution.py
+++ b/solution.py
@@ -324,12 +324,13 @@
             part = slice(f * FC, (f + 1) * FC)
             pre = jnp.dot(wint[part, :], normed_b, preferred_element_type=f32)
             ga = jnp.dot(wout[part, :], up, preferred_element_type=f32)
+            pre, ga = pre.astype(bf), ga.astype(bf)
             sq = pre * pre
             tangent = jnp.tanh(pre * (gelu_scale + (gelu_scale * cubic_coef) * sq))
             gate = 0.5 + 0.5 * tangent
             slope = gate + pre * (gate * (1.0 - tangent)) * (gelu_scale + (3.0 * gelu_scale * cubic_coef) * sq)
-            act[part, here] = (pre * gate).astype(bf)
-            gp[part, here] = (ga * slope).astype(bf)
+            act[part, here] = pre * gate
+            gp[part, here] = ga * slope
         gn = jnp.dot(win[...], gp[:, here], preferred_element_type=f32)
         for b in range(W // 128):
             part = slice(b * 128, (b + 1) * 128)
@@ -475,8 +476,8 @@
     kt[me_l] = total[0:16]
     start([rcopy(kt.at[me_l], kr.at[me_l - (me_l > l).astype(jnp.int32)], kt_s, kt_r, l, me_j) for l in loop_peers])
 
+    start(br_copies(1))
     halving(2)
-    start(br_copies(1))
     start(br_copies(2))
     halving(3)
     start(br_copies(3))

time: 38.7 us -> 37.8 us (0.977)
  Pallas kernels: 37.9 us -> 37 us
    pallas_call x1, Pallas kernels: 36.9 us -> 36 us  [fused_shards(): pl.pallas_call(functools.partial(fused_kernel, L, J, 1.0 / math.sqrt(rows...]
where the time goes in v7:
time: 37.8 us; the launch traced here: 37.7 us
  Pallas kernels  37 us (98%)
  between operations  0.64 us (2%)
    pallas_call x1, Pallas kernels, fused_shards(): pl.pallas_call(functools.partial(fused_kernel, L, J, 1.0 / math.sqrt(rows...  36 us
    pallas_call x1, Pallas kernels, fused_shards(): pl.pallas_call(flush_kernel, out_shape=shapes, in_specs=[pl.BlockSpec(mem...  1.02 us

profile of v7, /device:TPU:0, one launch (start us, length us, event | category | flops | bytes accessed | tf_op | source)
XLA Modules:
  0.0 37.7 jit_solution(10900270466666743323)
XLA Ops:
  0.6 36.0 %shard_map.92 = (bf16[64,4096]{1,0:T(8,128)(2,1)S(1)}, bf16[64,4096]{1,0:T(8,128)(2,1)S(1)}, f32[64,128]{1,0:T(8,128)S(1)}, f32[64,128]{1,0:T(8,128)S(1)}, f32[9,64]{1,0:T(8,128)S(1)}) custom-call(bf16[64,4096]{1,0:T(8,128)(2,1)} %bitcast.5, bf16[64,4096]{1,0:T(8,128)(2,1)} %bitcast.6, f32[9,64]{1,0:T(8,128)} %taps_hbm.1, bf16[256,1024]{1,0:T(8,128)(2,1)} %win_hbm.1, ...), custom_call_target="tpu_custom_call" | custom-call | flops 3221225472 | bytes 4194304 | tf_op jit(solution)/shard_map/pallas_call | solution.py:594
  36.6 1.0 %shard_map.93 = (bf16[64,4096]{1,0:T(8,128)(2,1)}, bf16[64,4096]{1,0:T(8,128)(2,1)}, f32[64,128]{1,0:T(8,128)}, f32[64,128]{1,0:T(8,128)}, f32[9,64]{1,0:T(8,128)}) custom-call(bf16[64,4096]{1,0:T(8,128)(2,1)S(1)} %get-tuple-element.15.refs_0_, bf16[64,4096]{1,0:T(8,128)(2,1)S(1)} %get-tuple-element.16.refs_1_, f32[64,128]{1,0:T(8,128)S(1)} %get-tuple-element.17.refs_2_, ...), custom_call_target="tpu_custom_call" | custom-call | tf_op jit(solution)/shard_map/pallas_call | solution.py:605

commit v8 on v7

--- a/solution.py
+++ b/solution.py
@@ -340,12 +340,16 @@
             geb[s, :, part] = out.astype(bf)
         start(ge_copies(s))
         gep[:, own_col(s, me_j)] = geb[s, mine, :]
-        brb[s] = jnp.dot(woutt[...], act[:, here], preferred_element_type=f32).astype(bf)
+
+        return carry
+
+    lax.fori_loop(0, S, mlp_body, 0)
+
+    def send_branch(s, carry):
+        brb[s] = jnp.dot(woutt[...], act[:, lanes(s * W, W)], preferred_element_type=f32).astype(bf)
         brv[:, col(s, me_j)] = brb[s, mine, :]
-
+        start(br_copies(s))
         return carry
-
-    lax.fori_loop(0, S, mlp_body, 0)
 
     def forward(s):
         got(gep.at[:, 0:(J - 1) * W], ge_r + s)
@@ -385,7 +389,7 @@
 
         @pl.when(e == 2)
         def _():
-            forward(1)
+            forward(0)
 
         @pl.when(e >= 2)
         def _():
@@ -457,12 +461,12 @@
 
         lax.fori_loop(0, B // 128, part, 0)
 
-    forward(0)
     lax.fori_loop(0, Z, term_body, 0)
     core_sum(Z - 2)
+    core_sum(Z - 1)
+    forward(1)
     kernel_terms(0)
-    core_sum(Z - 1)
-    start(br_copies(0))
+    send_branch(0, 0)
     kernel_terms(1)
     forward(2)
     kernel_terms(2)
@@ -476,11 +480,11 @@
     kt[me_l] = total[0:16]
     start([rcopy(kt.at[me_l], kr.at[me_l - (me_l > l).astype(jnp.int32)], kt_s, kt_r, l, me_j) for l in loop_peers])
 
-    start(br_copies(1))
+    send_branch(1, 0)
     halving(2)
-    start(br_copies(2))
+    send_branch(2, 0)
     halving(3)
-    start(br_copies(3))
+    send_branch(3, 0)
     got(gep.at[:, 0:(S - 1) * 2 * B], gh_r)
     back(False)
     z_stage(0)

time: 37.8 us -> 37.4 us (0.989)
  Pallas kernels: 37 us -> 36.6 us
    pallas_call x1, Pallas kernels: 36 us -> 35.6 us  [fused_shards(): pl.pallas_call(functools.partial(fused_kernel, L, J, 1.0 / math.sqrt(rows...]
where the time goes in v8:
time: 37.4 us; the launch traced here: 37.3 us
  Pallas kernels  36.6 us (98%)
  between operations  0.64 us (2%)
    pallas_call x1, Pallas kernels, fused_shards(): pl.pallas_call(functools.partial(fused_kernel, L, J, 1.0 / math.sqrt(rows...  35.6 us
    pallas_call x1, Pallas kernels, fused_shards(): pl.pallas_call(flush_kernel, out_shape=shapes, in_specs=[pl.BlockSpec(mem...  1.02 us

profile of v8, /device:TPU:0, one launch (start us, length us, event | category | flops | bytes accessed | tf_op | source)
XLA Modules:
  0.0 37.3 jit_solution(16320122933628742823)
XLA Ops:
  0.6 35.6 %shard_map.92 = (bf16[64,4096]{1,0:T(8,128)(2,1)S(1)}, bf16[64,4096]{1,0:T(8,128)(2,1)S(1)}, f32[64,128]{1,0:T(8,128)S(1)}, f32[64,128]{1,0:T(8,128)S(1)}, f32[9,64]{1,0:T(8,128)S(1)}) custom-call(bf16[64,4096]{1,0:T(8,128)(2,1)} %bitcast.5, bf16[64,4096]{1,0:T(8,128)(2,1)} %bitcast.6, f32[9,64]{1,0:T(8,128)} %taps_hbm.1, bf16[256,1024]{1,0:T(8,128)(2,1)} %win_hbm.1, ...), custom_call_target="tpu_custom_call" | custom-call | flops 3221225472 | bytes 4194304 | tf_op jit(solution)/shard_map/pallas_call | solution.py:598
  36.3 1.0 %shard_map.93 = (bf16[64,4096]{1,0:T(8,128)(2,1)}, bf16[64,4096]{1,0:T(8,128)(2,1)}, f32[64,128]{1,0:T(8,128)}, f32[64,128]{1,0:T(8,128)}, f32[9,64]{1,0:T(8,128)}) custom-call(bf16[64,4096]{1,0:T(8,128)(2,1)S(1)} %get-tuple-element.15.refs_0_, bf16[64,4096]{1,0:T(8,128)(2,1)S(1)} %get-tuple-element.16.refs_1_, f32[64,128]{1,0:T(8,128)S(1)} %get-tuple-element.17.refs_2_, ...), custom_call_target="tpu_custom_call" | custom-call | tf_op jit(solution)/shard_map/pallas_call | solution.py:609

commit v9 on v8

--- a/solution.py
+++ b/solution.py
@@ -162,7 +162,7 @@
     x_hbm, ct_hbm, taps_hbm, win_hbm, wout_hbm,
     bo_out, gx_out, gw_in_out, gw_out_out, gk_out,
     xp, ctv, tapv, win, wout, wint, woutt, tf, fb, fr, ctf, nb, nrm, istd, act, gp,
-    geb, brb, gep, brv, gfull, gsend, grecv, s1s, s1r, s2s, s2r, uf, sb, tr, gka, kt, kr, acc_x,
+    geb, brb, gep, brv, gfull, gsend, grecv, s1s, s1r, s2s, s2r, uf, sb, tr, gka, kt, kr, acc_x, gab,
     load, send, recv,
 ):
     cl, rows = ctv.shape
@@ -306,6 +306,7 @@
 
     def mlp_body(s, carry):
         got(ctf.at[s, 0:V, :], ct_r + s)
+        gab[...] = jnp.dot(wout[...], ctf[s], preferred_element_type=f32).astype(bf)
         got(fr.at[s, 0:V, :], f_r + s)
         here = lanes(s * W, W)
         for b in range(W // 128):
@@ -318,13 +319,11 @@
             istd[:, part] = inv
             nb[:, lanes(s * W + b * 128, 128)] = normed.astype(bf)
         normed_b = nb[:, here]
-        up = ctf[s]
         FC = 256
         for f in range(F // FC):
             part = slice(f * FC, (f + 1) * FC)
             pre = jnp.dot(wint[part, :], normed_b, preferred_element_type=f32)
-            ga = jnp.dot(wout[part, :], up, preferred_element_type=f32)
-            pre, ga = pre.astype(bf), ga.astype(bf)
+            pre, ga = pre.astype(bf), gab[part, :]
             sq = pre * pre
             tangent = jnp.tanh(pre * (gelu_scale + (gelu_scale * cubic_coef) * sq))
             gate = 0.5 + 0.5 * tangent
@@ -584,6 +583,7 @@
         pltpu.VMEM((L, 16, 128), f32),
         pltpu.VMEM((L - 1, 16, 128), f32),
         pltpu.VMEM((cl, rows), f32),
+        pltpu.VMEM((F, W), bf),
     ]
     scratch += [pltpu.SemaphoreType.DMA((5,)), pltpu.SemaphoreType.DMA((11,)), pltpu.SemaphoreType.DMA((7 * S + 6,))]
     vmem = pl.BlockSpec(memory_space=pltpu.VMEM)

time: 37.4 us -> 37.4 us (level)
  no operation moved by 1% of the time
where the time goes in v9:
time: 37.4 us; the launch traced here: 37.3 us
  Pallas kernels  36.6 us (98%)
  between operations  0.64 us (2%)
    pallas_call x1, Pallas kernels, fused_shards(): pl.pallas_call(functools.partial(fused_kernel, L, J, 1.0 / math.sqrt(rows...  35.6 us
    pallas_call x1, Pallas kernels, fused_shards(): pl.pallas_call(flush_kernel, out_shape=shapes, in_specs=[pl.BlockSpec(mem...  1.02 us

profile of v9, /device:TPU:0, one launch (start us, length us, event | category | flops | bytes accessed | tf_op | source)
XLA Modules:
  0.0 37.3 jit_solution(10120981135005622792)
XLA Ops:
  0.6 35.6 %shard_map.92 = (bf16[64,4096]{1,0:T(8,128)(2,1)S(1)}, bf16[64,4096]{1,0:T(8,128)(2,1)S(1)}, f32[64,128]{1,0:T(8,128)S(1)}, f32[64,128]{1,0:T(8,128)S(1)}, f32[9,64]{1,0:T(8,128)S(1)}) custom-call(bf16[64,4096]{1,0:T(8,128)(2,1)} %bitcast.5, bf16[64,4096]{1,0:T(8,128)(2,1)} %bitcast.6, f32[9,64]{1,0:T(8,128)} %taps_hbm.1, bf16[256,1024]{1,0:T(8,128)(2,1)} %win_hbm.1, ...), custom_call_target="tpu_custom_call" | custom-call | flops 3221225472 | bytes 4194304 | tf_op jit(solution)/shard_map/pallas_call | solution.py:598
  36.3 1.0 %shard_map.93 = (bf16[64,4096]{1,0:T(8,128)(2,1)}, bf16[64,4096]{1,0:T(8,128)(2,1)}, f32[64,128]{1,0:T(8,128)}, f32[64,128]{1,0:T(8,128)}, f32[9,64]{1,0:T(8,128)}) custom-call(bf16[64,4096]{1,0:T(8,128)(2,1)S(1)} %get-tuple-element.15.refs_0_, bf16[64,4096]{1,0:T(8,128)(2,1)S(1)} %get-tuple-element.16.refs_1_, f32[64,128]{1,0:T(8,128)S(1)} %get-tuple-element.17.refs_2_, ...), custom_call_target="tpu_custom_call" | custom-call | tf_op jit(solution)/shard_map/pallas_call | solution.py:609

commit v10 on v9

--- a/solution.py
+++ b/solution.py
@@ -319,7 +319,7 @@
             istd[:, part] = inv
             nb[:, lanes(s * W + b * 128, 128)] = normed.astype(bf)
         normed_b = nb[:, here]
-        FC = 256
+        FC = 512
         for f in range(F // FC):
             part = slice(f * FC, (f + 1) * FC)
             pre = jnp.dot(wint[part, :], normed_b, preferred_element_type=f32)

time: 37.4 us -> 37.4 us (level)
  no operation moved by 1% of the time
where the time goes in v10:
time: 37.4 us; the launch traced here: 37.3 us
  Pallas kernels  36.6 us (98%)
  between operations  0.64 us (2%)
    pallas_call x1, Pallas kernels, fused_shards(): pl.pallas_call(functools.partial(fused_kernel, L, J, 1.0 / math.sqrt(rows...  35.6 us
    pallas_call x1, Pallas kernels, fused_shards(): pl.pallas_call(flush_kernel, out_shape=shapes, in_specs=[pl.BlockSpec(mem...  1.02 us

profile of v10, /device:TPU:0, one launch (start us, length us, event | category | flops | bytes accessed | tf_op | source)
XLA Modules:
  0.0 37.3 jit_solution(15841151986396111394)
XLA Ops:
  0.6 35.6 %shard_map.92 = (bf16[64,4096]{1,0:T(8,128)(2,1)S(1)}, bf16[64,4096]{1,0:T(8,128)(2,1)S(1)}, f32[64,128]{1,0:T(8,128)S(1)}, f32[64,128]{1,0:T(8,128)S(1)}, f32[9,64]{1,0:T(8,128)S(1)}) custom-call(bf16[64,4096]{1,0:T(8,128)(2,1)} %bitcast.5, bf16[64,4096]{1,0:T(8,128)(2,1)} %bitcast.6, f32[9,64]{1,0:T(8,128)} %taps_hbm.1, bf16[256,1024]{1,0:T(8,128)(2,1)} %win_hbm.1, ...), custom_call_target="tpu_custom_call" | custom-call | flops 3221225472 | bytes 4194304 | tf_op jit(solution)/shard_map/pallas_call | solution.py:598
  36.3 1.0 %shard_map.93 = (bf16[64,4096]{1,0:T(8,128)(2,1)}, bf16[64,4096]{1,0:T(8,128)(2,1)}, f32[64,128]{1,0:T(8,128)}, f32[64,128]{1,0:T(8,128)}, f32[9,64]{1,0:T(8,128)}) custom-call(bf16[64,4096]{1,0:T(8,128)(2,1)S(1)} %get-tuple-element.15.refs_0_, bf16[64,4096]{1,0:T(8,128)(2,1)S(1)} %get-tuple-element.16.refs_1_, f32[64,128]{1,0:T(8,128)S(1)} %get-tuple-element.17.refs_2_, ...), custom_call_target="tpu_custom_call" | custom-call | tf_op jit(solution)/shard_map/pallas_call | solution.py:609
